TPU v7x, 128 devices: a whole 4x4x4 slice. The times are simulated.
128 devices in a mesh: lon: 16 (over x, y), lat: 8 (over z, core).
Axes of the slice: x: 4, y: 4, z: 4, core: 2. Of those that a mesh axis runs over, the one named last changes fastest.
Arguments:
- control: float32 [5, 127, 64, 2048], P(None, None, 'lat', 'lon'), may hold values from -6 to 6
- residual: float32 [5, 127, 64, 2048], P(None, None, 'lat', 'lon'), may hold values from -11 to 11
- direction: float32 [5, 127, 64, 2048], P(None, None, 'lat', 'lon'), may hold values from -11 to 11
- ensemble: bfloat16 [4, 2, 127, 64, 2048], P(None, None, None, 'lat', 'lon'), may hold values from -3 to 3
- static_std: bfloat16 [127, 64, 2048], P(None, 'lat', 'lon'), may hold values from 0.29882812 to 3
- vertical: float32 [127, 127], replicated, may hold values from 0 to 1
- owner: int32 [32768, 1], P(('lon', 'lat')), may hold values from 0 to 127; in each aligned block of 256 rows (0 to 255, 256 to 511, ...) at most 4 rows name the same one
- column: int32 [32768], P(('lon', 'lat')), may hold values from 0 to 894, as said below
- slot: int32 [32768], P(('lon', 'lat')), may hold values from 0 to 1
- corner: int32 [32768, 4], P(('lon', 'lat')), may hold values from 0 to 1, as said below
- obs_weight: float32 [32768, 127], P(('lon', 'lat')), may hold values from 0.2 to 2
- live_count: int32 [128], P(('lon', 'lat')), may hold values from 192 to 256
Outputs:
- new_control: float32 [5, 127, 64, 2048], P(None, None, 'lat', 'lon')
- new_residual: float32 [5, 127, 64, 2048], P(None, None, 'lat', 'lon')
- new_direction: float32 [5, 127, 64, 2048], P(None, None, 'lat', 'lon')
Inputs may be any that keep to these rules, and one draw needn't show every extreme that they name: `owner`: within the 256 records of one device no tile is named more than 4 times. `column`: the latitude row is below 7 and the longitude cell below 127. `corner`: exactly one entry of each row is 1.
All inputs are finite; a program needn't handle non-finite values.
Results may differ from a plain program's by a relative error of at most 0.0003.
Values sent between devices are 32-bit elements; how exact they have to be, the bound alone decides.
A program may use at most 128 MiB of HBM per device.

v0:
```python
import math

import jax
import jax.numpy as jnp
from jax import lax
from jax.sharding import PartitionSpec as P


def extended_2(array, sides, width, wrap):
    for axis, dim in sides:
        size, length = (lax.axis_size(axis), array.shape[dim])
        up = [(i, (i + 1) % size) for i in range(size if wrap else size - 1)]
        down = [(j, i) for i, j in up]
        last = lax.slice_in_dim(array, length - width, length, axis=dim)
        initial = lax.slice_in_dim(array, 0, width, axis=dim)
        before = lax.ppermute(last, axis, up)
        after = lax.ppermute(initial, axis, down)
        array = jnp.concatenate([before, array, after], axis=dim)
    return array


def filter_taps():
    raw_taps = [math.exp(-(offset * offset) / 8.0) for offset in range(-3, 4)]
    scale_total = math.sqrt(sum((entry_value * entry_value for entry_value in raw_taps)))
    return [entry_value / scale_total for entry_value in raw_taps]


def vertical_apply(matrix, field):
    return jnp.einsum("ab,kbij->kaij", matrix, field, precision=lax.Precision.HIGHEST)


def vertical_adjoint(matrix, field):
    return jnp.einsum("ba,kbij->kaij", matrix, field, precision=lax.Precision.HIGHEST)


def shift_sum(extended, width, axis_dim):
    taps = filter_taps()
    result = None
    for number, offset in enumerate(range(-3, 4)):
        term = taps[number] * lax.slice_in_dim(
            extended, 3 + offset, 3 + offset + width, axis=axis_dim
        )
        result = term if result is None else result + term
    return result


def smooth_field(field):
    lat_cells = field.shape[2]
    lon_cells = field.shape[3]
    extended = extended_2(field, (("lon", 3),), 3, True)
    across = shift_sum(extended, lon_cells, 3)
    padded = extended_2(across, (("lat", 2),), 3, False)
    return shift_sum(padded, lat_cells, 2)


def on_device(
    control,
    residual,
    direction,
    ensemble,
    static_std,
    vertical,
    owner,
    column,
    slot,
    corner,
    obs_weight,
    live_count,
):
    members = ensemble.shape[0]
    slots_count = ensemble.shape[1]
    levels = ensemble.shape[2]
    lat_cells = control.shape[2]
    lon_cells = control.shape[3]
    tile_cells = lat_cells * lon_cells
    devices = lax.axis_size(("lon", "lat"))
    record_count = owner.shape[0]
    capacity = max(2, 2 * record_count // devices)
    tile_ids = owner[:, 0]
    hits = (tile_ids[:, None] == jnp.arange(devices, dtype=jnp.int32)[None, :]).astype(jnp.int32)
    rank = jnp.sum(jnp.cumsum(hits, axis=0) * hits, axis=1) - 1
    live = jnp.arange(record_count, dtype=jnp.int32) < live_count[0]
    target = jnp.where(live, tile_ids * capacity + rank, devices * capacity)
    offsets = jnp.array([0, 1, lon_cells, lon_cells + 1], dtype=jnp.int32)
    place = slot * tile_cells + column + jnp.sum(corner * offsets, axis=1)
    place_buf = (
        jnp.full((devices * capacity,), -1.0, jnp.float32)
        .at[target]
        .set(place.astype(jnp.float32), mode="drop")
    )
    weight_buf = (
        jnp.zeros((devices * capacity, levels), jnp.float32).at[target].set(obs_weight, mode="drop")
    )
    weight_in, place_in = (
        lax.all_to_all(
            weight_buf.reshape(devices, capacity, levels),
            ("lon", "lat"),
            split_axis=0,
            concat_axis=0,
            tiled=True,
        ),
        lax.all_to_all(
            place_buf.reshape(devices, capacity),
            ("lon", "lat"),
            split_axis=0,
            concat_axis=0,
            tiled=True,
        ),
    )
    localized = smooth_field(vertical_apply(vertical, direction))
    increment = ensemble[0].astype(jnp.float32) * localized[0]
    for member in range(1, members):
        increment = increment + ensemble[member].astype(jnp.float32) * localized[member]
    spread = static_std.astype(jnp.float32)
    increment = increment + 0.5 * spread * localized[members]
    received = devices * capacity
    place_ids = place_in.reshape(received).astype(jnp.int32)
    table = (
        place_ids[:, None] == jnp.arange(slots_count * tile_cells, dtype=jnp.int32)[None, :]
    ).astype(jnp.float32)
    table = table.reshape(received, slots_count, tile_cells)
    flat_inc = increment.reshape(slots_count, levels, tile_cells)
    evolved = jnp.einsum("tlc,rtc->rl", flat_inc, table, precision=lax.Precision.HIGHEST)
    weighted = weight_in.reshape(received, levels) * evolved
    back = jnp.einsum("rtc,rl->tlc", table, weighted, precision=lax.Precision.HIGHEST)
    back = back.reshape(slots_count, levels, lat_cells, lon_cells)
    members_adj = [
        jnp.sum(ensemble[member].astype(jnp.float32) * back, axis=0) for member in range(members)
    ]
    members_adj.append(0.5 * spread * jnp.sum(back, axis=0))
    adjoint = jnp.stack(members_adj)
    image = direction + smooth_field(vertical_adjoint(vertical, adjoint))
    norm_now = lax.psum(jnp.sum(residual * residual), ("lon", "lat"))
    curve = lax.psum(jnp.sum(direction * image), ("lon", "lat"))
    alpha = norm_now / curve
    new_residual = residual - alpha * image
    norm_next = lax.psum(jnp.sum(new_residual * new_residual), ("lon", "lat"))
    new_control = control + alpha * direction
    new_direction = new_residual + norm_next / norm_now * direction
    return (new_control, new_residual, new_direction)


def solution(mesh):
    return jax.shard_map(
        on_device,
        mesh=mesh,
        in_specs=(
            P(None, None, "lat", "lon"),
            P(None, None, "lat", "lon"),
            P(None, None, "lat", "lon"),
            P(None, None, None, "lat", "lon"),
            P(None, "lat", "lon"),
            P(),
            P(("lon", "lat"), None),
            P(("lon", "lat")),
            P(("lon", "lat")),
            P(("lon", "lat"), None),
            P(("lon", "lat"), None),
            P(("lon", "lat")),
        ),
        out_specs=(
            P(None, None, "lat", "lon"),
            P(None, None, "lat", "lon"),
            P(None, None, "lat", "lon"),
        ),
        check_vma=False,
    )
```

profile of v0, /device:TPU:1, one launch (start us, length us, event | category | flops | bytes accessed | tf_op | source)
XLA Modules:
  0.0 318.0 jit_solution(5776957256541914640)
XLA Ops:
  0.6 2.6 copy.76
  3.3 2.3 convolution_bitcast_fusion.1
  5.6 1.5 copy-done.4
  7.2 2.2 collective-permute-start
  9.4 3.7 %collective-permute-start.1 = (f32[5,127,8,3]{1,3,2,0:T(4,128)S(1)}, f32[5,127,8,3]{1,3,2,0:T(4,128)S(1)}, u32[]{:S(2)}, u32[]{:S(2)}) collective-permute-start(f32[5,127,8,3]{1,3,2,0:T(4,128)S(1)} %get-tuple-element.36), channel_id=1, source_target_pairs={{8,0},{16,8},{24,16},{32,24},{40,32},{48,40},{56,48},{64,56},{72,6... | collective-permute-start | bytes 182888 | tf_op jit(solution)/shard_map/ppermute | solution.py:17
  13.7 1.1 collective-permute-done
  14.8 9.6 %fusion.21 = f32[5,127,8,128]{1,3,2,0:T(8,128)S(1)} fusion(f32[5,127,8,128]{1,3,2,0:T(8,128)} %copy-done.4, f32[5,127,8,3]{1,3,2,0:T(4,128)S(1)} %collective-permute-done.1, f32[5,127,8,3]{1,3,2,0:T(4,128)S(1)} %collective-permute-done), kind=kLoop, calls=%fused_computation.55 | loop fusion | flops 12354560 | bytes 5323840 | tf_op jit(solution)/shard_map/add | solution.py:43
  24.5 1.5 copy-done.2
  26.0 1.5 fusion.118
  27.5 5.2 %collective-permute-start.2 = (f32[5,127,3,128]{1,3,2,0:T(8,128)}, f32[5,127,3,128]{1,3,2,0:T(8,128)}, u32[]{:S(2)}, u32[]{:S(2)}) collective-permute-start(f32[5,127,3,128]{1,3,2,0:T(8,128)} %get-tuple-element.33), channel_id=1, source_target_pairs={{0,1},{1,2},{2,3},{3,4},{4,5},{5,6},{6,7},{8,9},{9,10},{10,11},{11... | collective-permute-start | bytes 2926088 | tf_op jit(solution)/shard_map/ppermute | solution.py:16
  32.7 1.9 collective-permute-start.3
  35.4 1.4 scatter_custom_fusion.1
  36.9 0.7 all_to_all.10
  37.6 9.9 %all-to-all-start.1 = ((f32[128,1,4]{2,1,0:T(1,128)}), f32[128,1,4]{2,1,0:T(1,128)S(1)}, u32[]{:S(2)}, u32[]{:S(2)}) async-start(f32[128,1,4]{2,1,0:T(1,128)} %bitcast.11), calls=%async_computation.1 | async-start | bytes 131072 | tf_op jit(solution)/shard_map/all_to_all | solution.py:102
  47.5 2.9 fusion.120
  50.4 0.3 copy.63
  50.6 1.4 copy.88
  52.1 2.2 copy.89
  54.3 2.2 copy.90
  56.5 2.2 copy.91
  58.6 1.2 copy.66
  59.9 2.3 copy.68
  62.1 2.3 copy.70
  64.4 2.3 copy.72
  66.6 2.2 scatter_custom_fusion
  68.8 10.2 %all-to-all-start = ((f32[128,4,127]{2,1,0:T(4,128)}), f32[128,4,127]{2,1,0:T(4,128)}, u32[]{:S(2)}, u32[]{:S(2)}) async-start(f32[128,4,127]{2,1,0:T(4,128)} %bitcast.86), calls=%async_computation | async-start | bytes 524288 | tf_op jit(solution)/shard_map/all_to_all | solution.py:95
  79.1 0.8 convert_reduce_fusion
  79.9 0.9 convert_element_type.63
  80.9 8.5 %fusion.50 = f32[5,127,8,128]{1,3,2,0:T(8,128)S(1)} fusion(f32[5,127,8,128]{1,3,2,0:T(8,128)} %copy-done.2, f32[5,127,3,128]{1,3,2,0:T(8,128)} %collective-permute-done.3, f32[5,127,3,128]{1,3,2,0:T(8,128)} %collective-permute-done.2), kind=kLoop, calls=%fused_computation.84 | loop fusion | flops 12354560 | bytes 7152640 | tf_op jit(solution)/shard_map/add | solution.py:43
  89.4 1.4 fusion.117
  90.8 0.8 fusion.93
  91.6 4.7 %fusion.82 = f32[512,127,1]{1,0,2:T(8,128)S(1)} fusion(f32[512,127]{1,0:T(8,128)} %bitcast.10, s32[2,1024]{1,0:T(2,128)S(1)} %multiply_add_fusion.2, s32[512]{0:T(512)S(1)} %convert_element_type.63, f32[127,1024]{0,1:T(8,128)} %bitcast.76, f32[127,1024]{0,1:T(8,128)} %bitcast.83, f32[127,1024]{0,1:T(8,128)} %bitcast.84, f32[127,1024]{0,1:T(8,128)} %bitcast.85, ...), kind=kOutput, calls=%fused_computation.126 | convolution fusion | flops 1602264576 | bytes 5212160 | tf_op jit(solution)/shard_map/tlc,rtc->rl/dot_general | solution.py:123
  96.4 3.3 %fusion.113 = (f32[127,1024]{1,0:T(8,128)S(1)}, f32[127,1024]{1,0:T(8,128)}, f32[127,1024]{1,0:T(8,128)}, f32[127,1024]{1,0:T(8,128)}, f32[127,1024]{1,0:T(8,128)}) fusion(f32[2,127,1024]{2,1,0:T(8,128)S(1)} %copy-done.9, f32[2,127,1024]{2,1,0:T(8,128)S(1)} %copy-done.8, f32[2,127,1024]{2,1,0:T(8,128)S(1)} %copy-done.7, f32[2,127,1024]{2,1,0:T(8,128)S(1)} %copy-done.6, ...), kind=kOutput, calls=%fused_computation.178 | convolution fusion | flops 1600769024 | bytes 7032832 | tf_op jit(solution)/shard_map/rtc,rl->tlc/dot_general | solution.py:125
  99.7 2.1 copy.67
  101.8 1.9 constant_dynamic-update-slice_fusion.3
  103.7 2.1 copy.69
  105.7 2.0 copy.71
  107.8 2.0 copy.73
  109.8 1.0 copy.74
  110.8 1.9 constant_dynamic-update-slice_fusion.2
  112.8 1.9 constant_dynamic-update-slice_fusion.1
  114.7 1.9 constant_dynamic-update-slice_fusion
  116.6 0.9 bitcast_dynamic-update-slice_fusion
  117.4 4.0 %convolution_bitcast_fusion = f32[5,127,8,128]{1,3,2,0:T(8,128)S(1)} fusion(f32[5,127,8,128]{1,3,2,0:T(8,128)} %bitcast_dynamic-update-slice_fusion, f32[127,127]{1,0:T(8,128)S(1)} %copy-done), kind=kOutput, calls=%fused_computation.121 | convolution fusion | flops 990965760 | bytes 5266436 | tf_op jit(solution)/shard_map/ba,kbij->kaij/dot_general | solution.py:33
  121.5 1.5 collective-permute-start.4
  123.0 3.5 %collective-permute-start.5 = (f32[5,127,8,3]{1,3,2,0:T(4,128)S(1)}, f32[5,127,8,3]{1,3,2,0:T(4,128)S(1)}, u32[]{:S(2)}, u32[]{:S(2)}) collective-permute-start(f32[5,127,8,3]{1,3,2,0:T(4,128)S(1)} %get-tuple-element.28), channel_id=1, source_target_pairs={{8,0},{16,8},{24,16},{32,24},{40,32},{48,40},{56,48},{64,56},{72,6... | collective-permute-start | bytes 182888 | tf_op jit(solution)/shard_map/ppermute | solution.py:17
  126.5 1.7 collective-permute-done.4
  128.2 2.7 fusion.7
  130.9 1.5 copy-done.3
  132.4 1.5 fusion.115
  133.9 4.8 %collective-permute-start.6 = (f32[5,127,3,128]{1,3,2,0:T(8,128)}, f32[5,127,3,128]{1,3,2,0:T(8,128)}, u32[]{:S(2)}, u32[]{:S(2)}) collective-permute-start(f32[5,127,3,128]{1,3,2,0:T(8,128)} %get-tuple-element.25), channel_id=1, source_target_pairs={{0,1},{1,2},{2,3},{3,4},{4,5},{5,6},{6,7},{8,9},{9,10},{10,11},{11... | collective-permute-start | bytes 2926088 | tf_op jit(solution)/shard_map/ppermute | solution.py:16
  138.7 2.1 collective-permute-start.7
  140.9 3.4 %copy.79 = f32[5,127,8,128]{1,3,2,0:T(8,128)} copy(f32[5,127,8,128]{3,2,1,0:T(8,128)} %param.14) | data formatting | bytes 5201920 | tf_op args[1]
  144.3 3.4 %copy.78 = f32[5,127,8,128]{1,3,2,0:T(8,128)} copy(f32[5,127,8,128]{3,2,1,0:T(8,128)} %param.13) | data formatting | bytes 5201920 | tf_op args[0]
  147.7 3.0 multiply_reduce_fusion.2
  150.7 3.7 %collective-permute-done.7 = f32[5,127,3,128]{1,3,2,0:T(8,128)} collective-permute-done((f32[5,127,3,128]{1,3,2,0:T(8,128)}, f32[5,127,3,128]{1,3,2,0:T(8,128)}, u32[]{:S(2)}, u32[]{:S(2)}) %collective-permute-start.7) | collective-permute-done | bytes 975392 | tf_op jit(solution)/shard_map/ppermute | solution.py:17
  154.4 10.4 %multiply_reduce_fusion.1 = (f32[]{:T(128)}, f32[5,127,8,128]{1,3,2,0:T(8,128)}) fusion(f32[5,127,8,128]{1,3,2,0:T(8,128)S(1)} %copy.76, f32[5,127,3,128]{1,3,2,0:T(8,128)} %collective-permute-done.7, f32[5,127,8,128]{1,3,2,0:T(8,128)} %copy-done.3, f32[5,127,3,128]{1,3,2,0:T(8,128)} %collective-permute-done.6), kind=kLoop, calls=%fused_computation.115 | loop fusion | flops 14305279 | bytes 9753604 | tf_op jit(solution)/shard_map/reduce_sum | solution.py:134
  164.8 65.7 %all-reduce = (f32[]{:T(128)}, f32[]{:T(128)}) all-reduce(f32[]{:T(128)} %multiply_reduce_fusion.2, f32[]{:T(128)} %get-tuple-element.21), channel_id=1, replica_groups=mesh['lon'=16,'lat'=8] {'lon','lat'}, use_global_device_ids=true, to_apply=%region_1.2 | all-reduce | flops 2 | bytes 16 | tf_op jit(solution)/shard_map/psum | solution.py:133
  231.8 5.6 %multiply_reduce_fusion = (f32[]{:T(128)}, f32[5,127,8,128]{1,3,2,0:T(8,128)}) fusion(f32[5,127,8,128]{1,3,2,0:T(8,128)} %copy.79, f32[5,127,8,128]{1,3,2,0:T(8,128)} %get-tuple-element.22, f32[]{:T(128)S(6)} %div.6), kind=kLoop, calls=%fused_computation.112 | loop fusion | flops 2600959 | bytes 7802888 | tf_op jit(solution)/shard_map/reduce_sum | solution.py:137
  237.4 63.9 %psum.23 = f32[]{:T(128)} all-reduce(f32[]{:T(128)} %get-tuple-element.19), channel_id=1, replica_groups=mesh['lon'=16,'lat'=8] {'lon','lat'}, use_global_device_ids=true, to_apply=%region_16.17 | all-reduce | flops 1 | bytes 8 | tf_op jit(solution)/shard_map/psum | solution.py:137
  302.6 3.4 %copy.82 = f32[5,127,8,128]{3,2,1,0:T(8,128)} copy(f32[5,127,8,128]{1,3,2,0:T(8,128)} %get-tuple-element.20) | data formatting | bytes 5201920
  306.0 6.2 %multiply_add_fusion = (f32[5,127,8,128]{1,3,2,0:T(8,128)}, f32[5,127,8,128]{1,3,2,0:T(8,128)}) fusion(f32[5,127,8,128]{1,3,2,0:T(8,128)} %get-tuple-element.20, f32[5,127,8,128]{1,3,2,0:T(8,128)S(1)} %copy.76, f32[]{:T(128)S(6)} %div.7, f32[5,127,8,128]{1,3,2,0:T(8,128)} %copy.78, f32[]{:T(128)S(6)} %div.6), kind=kLoop, calls=%fused_computation.111 | loop fusion | flops 2600960 | bytes 13004808 | tf_op jit(solution)/shard_map/add | solution.py:139
  312.2 3.6 %copy.81 = f32[5,127,8,128]{3,2,1,0:T(8,128)} copy(f32[5,127,8,128]{1,3,2,0:T(8,128)} %get-tuple-element.24) | data formatting | bytes 5201920
  315.7 2.2 copy.83
  (54 shorter events, 0.8 us)
Async XLA Ops:
  0.6 2.7 copy-start
  3.3 9.8 %copy-start.12 = (s32[256,1]{0,1:T(1,128)S(1)}, s32[256,1]{0,1:T(1,128)}, u32[]{:S(2)}) copy-start(s32[256,1]{0,1:T(1,128)} %param.19) | copy-start | bytes 3076
  5.6 1.5 copy-start.4
  7.2 7.7 %collective-permute-start = (f32[5,127,8,3]{1,3,2,0:T(4,128)S(1)}, f32[5,127,8,3]{1,3,2,0:T(4,128)S(1)}, u32[]{:S(2)}, u32[]{:S(2)}) collective-permute-start(f32[5,127,8,3]{1,3,2,0:T(4,128)S(1)} %get-tuple-element.35), channel_id=1, source_target_pairs={{0,8},{8,16},{16,24},{24,32},{32,40},{40,48},{48,56},{56,64},{64,7... | collective-permute-start | bytes 182888 | tf_op jit(solution)/shard_map/ppermute | solution.py:16
  9.4 5.5 %collective-permute-start.1 = (f32[5,127,8,3]{1,3,2,0:T(4,128)S(1)}, f32[5,127,8,3]{1,3,2,0:T(4,128)S(1)}, u32[]{:S(2)}, u32[]{:S(2)}) collective-permute-start(f32[5,127,8,3]{1,3,2,0:T(4,128)S(1)} %get-tuple-element.36), channel_id=1, source_target_pairs={{8,0},{16,8},{24,16},{32,24},{40,32},{48,40},{56,48},{64,56},{72,6... | collective-permute-start | bytes 182888 | tf_op jit(solution)/shard_map/ppermute | solution.py:17
  24.5 1.5 copy-start.2
  26.0 8.7 %copy-start.13 = (s32[256,4]{0,1:T(4,128)S(1)}, s32[256,4]{0,1:T(4,128)}, u32[]{:S(2)}) copy-start(s32[256,4]{0,1:T(4,128)} %param.22) | copy-start | bytes 12292
  26.0 8.7 %copy-start.16 = (s32[4]{0:T(128)S(1)}, s32[4]{0:T(128)}, u32[]{:S(2)}) copy-start(s32[4]{0:T(128)} %constant.35.clone) | copy-start | bytes 52
  26.0 9.4 %copy-start.14 = (s32[256]{0:T(256)S(1)}, s32[256]{0:T(256)}, u32[]{:S(2)}) copy-start(s32[256]{0:T(256)} %param.20) | copy-start | bytes 3076
  26.0 9.5 %copy-start.15 = (s32[256]{0:T(256)S(1)}, s32[256]{0:T(256)}, u32[]{:S(2)}) copy-start(s32[256]{0:T(256)} %param.21) | copy-start | bytes 3076
  27.5 22.9 %copy-start.11 = (bf16[127,8,128]{2,1,0:T(8,128)(2,1)S(1)}, bf16[127,8,128]{2,1,0:T(8,128)(2,1)}, u32[]{:S(2)}) copy-start(bf16[127,8,128]{2,1,0:T(8,128)(2,1)} %param.17) | copy-start | bytes 780292
  27.5 53.4 %collective-permute-start.2 = (f32[5,127,3,128]{1,3,2,0:T(8,128)}, f32[5,127,3,128]{1,3,2,0:T(8,128)}, u32[]{:S(2)}, u32[]{:S(2)}) collective-permute-start(f32[5,127,3,128]{1,3,2,0:T(8,128)} %get-tuple-element.33), channel_id=1, source_target_pairs={{0,1},{1,2},{2,3},{3,4},{4,5},{5,6},{6,7},{8,9},{9,10},{10,11},{11... | collective-permute-start | bytes 2926088 | tf_op jit(solution)/shard_map/ppermute | solution.py:16
  32.7 48.1 %collective-permute-start.3 = (f32[5,127,3,128]{1,3,2,0:T(8,128)}, f32[5,127,3,128]{1,3,2,0:T(8,128)}, u32[]{:S(2)}, u32[]{:S(2)}) collective-permute-start(f32[5,127,3,128]{1,3,2,0:T(8,128)} %get-tuple-element.34), channel_id=1, source_target_pairs={{1,0},{2,1},{3,2},{4,3},{5,4},{6,5},{7,6},{9,8},{10,9},{11,10},{12... | collective-permute-start | bytes 2926088 | tf_op jit(solution)/shard_map/ppermute | solution.py:17
  37.6 31.3 %all-to-all-start.1 = ((f32[128,1,4]{2,1,0:T(1,128)}), f32[128,1,4]{2,1,0:T(1,128)S(1)}, u32[]{:S(2)}, u32[]{:S(2)}) async-start(f32[128,1,4]{2,1,0:T(1,128)} %bitcast.11), calls=%async_computation.1 | async-start | bytes 131072 | tf_op jit(solution)/shard_map/all_to_all | solution.py:102
  68.8 22.8 %all-to-all-start = ((f32[128,4,127]{2,1,0:T(4,128)}), f32[128,4,127]{2,1,0:T(4,128)}, u32[]{:S(2)}, u32[]{:S(2)}) async-start(f32[128,4,127]{2,1,0:T(4,128)} %bitcast.86), calls=%async_computation | async-start | bytes 524288 | tf_op jit(solution)/shard_map/all_to_all | solution.py:95
  91.6 4.8 %copy-start.6 = (f32[2,127,1024]{2,1,0:T(8,128)S(1)}, f32[2,127,1024]{2,1,0:T(8,128)}, u32[]{:S(2)}) copy-start(f32[2,127,1024]{2,1,0:T(8,128)} %copy.66) | copy-start | bytes 3121156
  91.6 4.8 %copy-start.7 = (f32[2,127,1024]{2,1,0:T(8,128)S(1)}, f32[2,127,1024]{2,1,0:T(8,128)}, u32[]{:S(2)}) copy-start(f32[2,127,1024]{2,1,0:T(8,128)} %copy.68) | copy-start | bytes 3121156
  91.6 4.8 %copy-start.8 = (f32[2,127,1024]{2,1,0:T(8,128)S(1)}, f32[2,127,1024]{2,1,0:T(8,128)}, u32[]{:S(2)}) copy-start(f32[2,127,1024]{2,1,0:T(8,128)} %copy.70) | copy-start | bytes 3121156
  91.6 4.8 %copy-start.9 = (f32[2,127,1024]{2,1,0:T(8,128)S(1)}, f32[2,127,1024]{2,1,0:T(8,128)}, u32[]{:S(2)}) copy-start(f32[2,127,1024]{2,1,0:T(8,128)} %copy.72) | copy-start | bytes 3121156
  110.8 5.7 %copy-start.10 = (f32[127,1024]{0,1:T(8,128)S(1)}, f32[127,1024]{0,1:T(8,128)}, u32[]{:S(2)}) copy-start(f32[127,1024]{0,1:T(8,128)} %copy.74) | copy-start | bytes 1560580
  121.5 6.7 %collective-permute-start.4 = (f32[5,127,8,3]{1,3,2,0:T(4,128)S(1)}, f32[5,127,8,3]{1,3,2,0:T(4,128)S(1)}, u32[]{:S(2)}, u32[]{:S(2)}) collective-permute-start(f32[5,127,8,3]{1,3,2,0:T(4,128)S(1)} %get-tuple-element.27), channel_id=1, source_target_pairs={{0,8},{8,16},{16,24},{24,32},{32,40},{40,48},{48,56},{56,64},{64,7... | collective-permute-start | bytes 182888 | tf_op jit(solution)/shard_map/ppermute | solution.py:16
  123.0 5.3 %collective-permute-start.5 = (f32[5,127,8,3]{1,3,2,0:T(4,128)S(1)}, f32[5,127,8,3]{1,3,2,0:T(4,128)S(1)}, u32[]{:S(2)}, u32[]{:S(2)}) collective-permute-start(f32[5,127,8,3]{1,3,2,0:T(4,128)S(1)} %get-tuple-element.28), channel_id=1, source_target_pairs={{8,0},{16,8},{24,16},{32,24},{40,32},{48,40},{56,48},{64,56},{72,6... | collective-permute-start | bytes 182888 | tf_op jit(solution)/shard_map/ppermute | solution.py:17
  130.9 1.5 copy-start.3
  133.9 16.8 %collective-permute-start.6 = (f32[5,127,3,128]{1,3,2,0:T(8,128)}, f32[5,127,3,128]{1,3,2,0:T(8,128)}, u32[]{:S(2)}, u32[]{:S(2)}) collective-permute-start(f32[5,127,3,128]{1,3,2,0:T(8,128)} %get-tuple-element.25), channel_id=1, source_target_pairs={{0,1},{1,2},{2,3},{3,4},{4,5},{5,6},{6,7},{8,9},{9,10},{10,11},{11... | collective-permute-start | bytes 2926088 | tf_op jit(solution)/shard_map/ppermute | solution.py:16
  138.7 15.7 %collective-permute-start.7 = (f32[5,127,3,128]{1,3,2,0:T(8,128)}, f32[5,127,3,128]{1,3,2,0:T(8,128)}, u32[]{:S(2)}, u32[]{:S(2)}) collective-permute-start(f32[5,127,3,128]{1,3,2,0:T(8,128)} %get-tuple-element.26), channel_id=1, source_target_pairs={{1,0},{2,1},{3,2},{4,3},{5,4},{6,5},{7,6},{9,8},{10,9},{11,10},{12... | collective-permute-start | bytes 2926088 | tf_op jit(solution)/shard_map/ppermute | solution.py:17
  312.2 3.6 %copy-start.5 = (f32[5,127,8,128]{1,3,2,0:T(8,128)S(1)}, f32[5,127,8,128]{1,3,2,0:T(8,128)}, u32[]{:S(2)}) copy-start(f32[5,127,8,128]{1,3,2,0:T(8,128)} %get-tuple-element.23) | copy-start | bytes 7802884
  312.2 5.8 %copy-start.1 = (f32[127,127]{1,0:T(8,128)S(1)}, f32[127,127]{1,0:T(8,128)}, u32[]{:S(2)}) copy-start(f32[127,127]{1,0:T(8,128)} %param.18) | copy-start | bytes 193552
where the time goes:
time: 319 us; the launch traced here: 318 us
  blocking collectives  130 us (41%)
  local copies, waits for them, and re-layouts  69 us (22%)
  other arithmetic  49 us (15%)
  starting transfers between devices  45.1 us (14%)
  matrix products  14.4 us (5%)
  waiting for transfers between devices  6.65 us (2%)
  between operations  4.33 us (1%)
    psum x1, blocking collectives, on_device(): norm_now = lax.psum(jnp.sum(residual * residual), ('lon', 'lat'))  65.7 us
    psum x1, blocking collectives, on_device(): norm_next = lax.psum(jnp.sum(new_residual * new_residual), ('lon', 'lat'))  63.9 us
    unnamed x50, local copies, waits for them, and re-layouts  39.1 us
    add x3, other arithmetic, shift_sum(): result = term if result is None else result + term  20.8 us
    ppermute x4, starting transfers between devices, extended_2(): before = lax.ppermute(last, axis, up)  13.7 us
    ppermute x4, starting transfers between devices, extended_2(): after = lax.ppermute(initial, axis, down)  11.3 us
    reduce_sum x1, other arithmetic, on_device(): curve = lax.psum(jnp.sum(direction * image), ('lon', 'lat'))  10.4 us
    all_to_all x1, starting transfers between devices, on_device(): lax.all_to_all(weight_buf.reshape(devices, capacity, levels), ('lon', 'la...  10.2 us
  transfers between devices with their start and end apart: 10, of which 3 were waited for; matrix products, arithmetic and copies ran while one was open for 14% of the time, Pallas kernels for 0%

commit v1 on v0

v1 whole, which is shorter than its diff:
```python
import math

import jax
import jax.numpy as jnp
from jax import lax
from jax.experimental import pallas as pl
from jax.experimental.pallas import tpu as pltpu
from jax.sharding import PartitionSpec as P

LEV = 127
COMPS = 5
MEMBERS = 4
ROWS = 8
CELLS = 128
TILE = LEV * ROWS
LAT = 8
LON = 16
RECORDS = 256
CAP = 4
F32 = jnp.float32
BF16 = jnp.bfloat16


def filter_taps():
    raw = [math.exp(-(offset * offset) / 8.0) for offset in range(-3, 4)]
    scale = math.sqrt(sum(value * value for value in raw))
    return [value / scale for value in raw[3:]]


def iota(shape, dim):
    return lax.broadcasted_iota(jnp.int32, shape, dim)


def split(value):
    high = value.astype(BF16)
    return high, (value - high.astype(F32)).astype(BF16)


def mxu(a, b):
    return lax.dot_general(a, b, (((1,), (0,)), ((), ())), preferred_element_type=F32)


def level_matrix(matrix):
    high, low = split(matrix)
    return jnp.concatenate(
        [jnp.concatenate([high, high], 1), jnp.concatenate([low, jnp.zeros_like(low)], 1)], 0
    )


def lane_matrix(matrix):
    high, low = split(matrix)
    return jnp.concatenate(
        [jnp.concatenate([high, low], 1), jnp.concatenate([high, jnp.zeros_like(low)], 1)], 0
    )


def level_product(matrix, field):
    high, low = split(field)
    both = mxu(matrix, jnp.concatenate([high, low], 0))
    return both[:CELLS] + both[CELLS:]


def lane_product(field, matrix):
    high, low = split(field)
    both = mxu(jnp.concatenate([high, low], 1), matrix)
    return both[:, :CELLS] + both[:, CELLS:]


def kernel(
    live_ref, owner_ref, column_ref, slot_ref, corner_ref, weight_ref, std_ref, v_ref,
    d_hbm, r_hbm, ens_hbm,
    out_hbm, scalars_ref,
    d_nat, r_nat, o_nat, ens16, ens, x_ref, y_ref, halo, lon_out, lon_in, lon_lev, inc, dens,
    vpad, level_w, lane_w, rec_out1, rec_in1, rec_out2, rec_in2, rec_t, part1, part2,
    load_sem, lon_send, lon_recv, lat_send, lat_recv,
    rec1_send, rec1_recv, rec2_send, rec2_recv, red1_send, red1_recv, red2_send, red2_recv,
):
    lon = lax.axis_index("lon")
    lat = lax.axis_index("lat")
    taps = filter_taps()
    lane = iota((CELLS, CELLS), 1)

    def lat_peer(o):
        return lax.rem(lat + o, LAT)

    def lon_peer(o):
        return lax.rem(lon + o, LON)

    east, west = lon_peer(1), lon_peer(LON - 1)

    def remote(src, dst, send, recv, axis, peer):
        return pltpu.make_async_remote_copy(
            src_ref=src, dst_ref=dst, send_sem=send, recv_sem=recv,
            device_id={axis: peer}, device_id_type=pl.DeviceIdType.MESH,
        )

    barrier = pltpu.get_barrier_semaphore()

    @pl.loop(1, LAT)
    def _(o):
        pl.semaphore_signal(
            barrier, inc=1, device_id={"lat": lat_peer(o)}, device_id_type=pl.DeviceIdType.MESH
        )

    @pl.loop(1, LON)
    def _(o):
        pl.semaphore_signal(
            barrier, inc=1, device_id={"lon": lon_peer(o)}, device_id_type=pl.DeviceIdType.MESH
        )

    d_load = pltpu.make_async_copy(d_hbm, d_nat.at[pl.ds(0, COMPS * TILE)], load_sem.at[0])
    ens_load = pltpu.make_async_copy(ens_hbm, ens16, load_sem.at[1])
    r_load = pltpu.make_async_copy(r_hbm, r_nat.at[pl.ds(0, COMPS * TILE)], load_sem.at[2])
    d_load.start()
    ens_load.start()
    r_load.start()

    zeros8 = jnp.zeros((ROWS, CELLS), F32)
    d_nat[COMPS * TILE:, :] = zeros8
    r_nat[COMPS * TILE:, :] = zeros8
    ens[9 * TILE:, :] = zeros8
    vpad[...] = jnp.zeros((CELLS, CELLS), F32)
    vpad[0:LEV, 0:LEV] = v_ref[...]
    level_w[0] = level_matrix(vpad[...])
    level_w[1] = level_matrix(vpad[...].T)
    gap = jnp.abs(iota((CELLS, CELLS), 0) - lane)
    inner = jnp.zeros((CELLS, CELLS), F32)
    wrapped = inner
    for k in range(4):
        inner = jnp.where(gap == k, taps[k], inner)
        if k:
            wrapped = jnp.where(gap == CELLS - k, taps[k], wrapped)
    lane_w[0] = lane_matrix(inner)
    lane_w[1] = lane_matrix(wrapped)

    eye = iota((RECORDS, RECORDS), 0) == iota((RECORDS, RECORDS), 1)
    before = iota((RECORDS, RECORDS), 0) < iota((RECORDS, RECORDS), 1)
    owner = owner_ref[...]
    owner_col = jnp.sum(jnp.where(eye, owner, 0), axis=1, keepdims=True)
    rank = jnp.sum(jnp.where((owner_col == owner) & before, 1, 0), axis=0, keepdims=True)
    corner = corner_ref[...]
    place = (
        slot_ref[...] * (ROWS * CELLS) + column_ref[...]
        + corner[1:2] + CELLS * corner[2:3] + (CELLS + 1) * corner[3:4]
    )
    place_col = jnp.sum(jnp.where(eye, place, 0), axis=1, keepdims=True).astype(F32)
    target = (((owner & (LAT - 1)) * LON + (owner >> 3)) * CAP) + rank
    target = jnp.where(iota((1, RECORDS), 1) < live_ref[0], target, -1)
    chosen = jnp.where(iota((LAT * LON * CAP, RECORDS), 0) == target, 1.0, 0.0).astype(BF16)
    weights = jnp.concatenate([weight_ref[...], place_col], 1)
    high = weights.astype(BF16)
    mid = (weights - high.astype(F32)).astype(BF16)
    packed = mxu(chosen, jnp.concatenate([high, mid], 1))
    packed = packed[:, :CELLS] + packed[:, CELLS:]
    for s in range(LAT):
        rec_out1[s] = packed[s * LON * CAP:(s + 1) * LON * CAP]

    def blank(side):
        @pl.loop(0, 2 * COMPS)
        def _(n):
            halo[n, side] = jnp.zeros((3, CELLS, CELLS), F32)

    @pl.when(lat == 0)
    def _():
        blank(0)

    @pl.when(lat == LAT - 1)
    def _():
        blank(1)

    def d_rows(q):
        k, i = q // ROWS, lax.rem(q, ROWS)
        return d_nat[pl.ds(k * TILE + i, CELLS, stride=ROWS), :]

    def x_rows(q):
        return x_ref[q]

    def pack_lon(phase, rows):
        def body(q, carry):
            left, right = carry
            value = rows(q)
            here = (lane >= 3 * q) & (lane < 3 * q + 3)
            left = jnp.where(here, pltpu.roll(value, 3 * q + 3, 1), left)
            right = jnp.where(here, pltpu.roll(value, 3 * q, 1), right)
            return left, right

        zero = jnp.zeros((CELLS, CELLS), F32)
        left, right = lax.fori_loop(0, COMPS * ROWS, body, (zero, zero))
        lon_out[phase, 0] = left
        lon_out[phase, 1] = right

    def lon_copies(phase):
        return [
            remote(lon_out.at[phase, 0], lon_in.at[phase, 0], lon_send.at[phase, 0],
                   lon_recv.at[phase, 0], "lon", east),
            remote(lon_out.at[phase, 1], lon_in.at[phase, 1], lon_send.at[phase, 1],
                   lon_recv.at[phase, 1], "lon", west),
        ]

    def lat_north(phase, k):
        n = phase * COMPS + k
        return remote(y_ref.at[pl.ds(k * ROWS, 3)], halo.at[n, 1], lat_send.at[n, 1],
                      lat_recv.at[n, 1], "lat", lax.rem(lat + LAT - 1, LAT))

    def lat_south(phase, k):
        n = phase * COMPS + k
        return remote(y_ref.at[pl.ds(k * ROWS + 5, 3)], halo.at[n, 0], lat_send.at[n, 0],
                      lat_recv.at[n, 0], "lat", lax.rem(lat + 1, LAT))

    def lat_start(phase, k):
        @pl.when(lat > 0)
        def _():
            lat_north(phase, k).start()

        @pl.when(lat < LAT - 1)
        def _():
            lat_south(phase, k).start()

    def lat_arrived(phase, k):
        @pl.when(lat > 0)
        def _():
            lat_south(phase, k).wait_recv()

        @pl.when(lat < LAT - 1)
        def _():
            lat_north(phase, k).wait_recv()

    def lat_sent(phase):
        @pl.loop(0, COMPS)
        def _(k):
            @pl.when(lat > 0)
            def _():
                lat_north(phase, k).wait_send()

            @pl.when(lat < LAT - 1)
            def _():
                lat_south(phase, k).wait_send()

    def own_part(phase, rows):
        @pl.loop(0, COMPS * ROWS // 2)
        def _(p):
            value = jnp.concatenate([rows(2 * p), rows(2 * p + 1)], 1)
            value = level_product(level_w[phase], value)
            value = jnp.concatenate([value[:, :CELLS], value[:, CELLS:]], 0)
            value = lane_product(value, lane_w[0])
            y_ref[2 * p] = value[:CELLS]
            y_ref[2 * p + 1] = value[CELLS:]

    def lon_part(phase):
        for copy in lon_copies(phase):
            copy.wait_recv()
        edges = jnp.concatenate([lon_in[phase, 0], lon_in[phase, 1]], 1)
        edges = level_product(level_w[phase], edges)
        lon_lev[0] = edges[:, :CELLS]
        lon_lev[1] = edges[:, CELLS:]

        def spread(q):
            left = pltpu.roll(lon_lev[0], CELLS - 3 - 3 * q, 1)
            right = pltpu.roll(lon_lev[1], lax.rem(CELLS - 3 * q, CELLS), 1)
            return jnp.where(lane >= CELLS // 2, left, right)

        @pl.loop(0, COMPS)
        def _(k):
            @pl.loop(0, ROWS // 2)
            def _(p):
                q = k * ROWS + 2 * p
                value = lane_product(jnp.concatenate([spread(q), spread(q + 1)], 0), lane_w[1])
                y_ref[q] += value[:CELLS]
                y_ref[q + 1] += value[CELLS:]

            lat_start(phase, k)

    def lat_rows(phase, k, c):
        part = pl.ds(c * 8, 8)
        n = phase * COMPS + k
        rows = [halo[n, 0, j, part] for j in range(3)]
        rows += [y_ref[k * ROWS + i, part] for i in range(ROWS)]
        rows += [halo[n, 1, j, part] for j in range(3)]
        out = []
        for i in range(ROWS):
            total = taps[0] * rows[i + 3]
            for j in range(1, 4):
                total = total + taps[j] * (rows[i + 3 - j] + rows[i + 3 + j])
            out.append(total)
        return out

    def ens_rows(plane, c, i):
        return ens[pl.ds(plane * TILE + c * 64 + i, 8, stride=ROWS), :]

    def reduce_first(n, height, value):
        part1[n, lat, 0:height] = value

        @pl.loop(1, LAT)
        def _(o):
            ref = part1.at[n, lat, pl.ds(0, height)]
            remote(ref, ref, red1_send.at[n, o], red1_recv.at[n, lat], "lat", lat_peer(o)).start()

    def reduce_second(n, height):
        @pl.loop(1, LAT)
        def _(o):
            ref = part1.at[n, lat_peer(o), pl.ds(0, height)]
            remote(ref, ref, red1_send.at[n, o], red1_recv.at[n, lat_peer(o)], "lat",
                   lat_peer(o)).wait_recv()

        total = part1[n, 0, 0:height]
        for s in range(1, LAT):
            total = total + part1[n, s, 0:height]
        part2[n, lon, 0:height] = total

        @pl.loop(1, LON)
        def _(o):
            ref = part2.at[n, lon, pl.ds(0, height)]
            remote(ref, ref, red2_send.at[n, o], red2_recv.at[n, lon], "lon", lon_peer(o)).start()

    def reduce_last(n, height):
        @pl.loop(1, LON)
        def _(o):
            ref = part2.at[n, lon_peer(o), pl.ds(0, height)]
            remote(ref, ref, red2_send.at[n, o], red2_recv.at[n, lon_peer(o)], "lon",
                   lon_peer(o)).wait_recv()

        total = part2[n, 0, 0:height]
        for s in range(1, LON):
            total = total + part2[n, s, 0:height]
        return total

    def reduce_sent(n, height):
        @pl.loop(1, LAT)
        def _(o):
            ref = part1.at[n, lat, pl.ds(0, height)]
            remote(ref, ref, red1_send.at[n, o], red1_recv.at[n, lat], "lat",
                   lat_peer(o)).wait_send()

        @pl.loop(1, LON)
        def _(o):
            ref = part2.at[n, lon, pl.ds(0, height)]
            remote(ref, ref, red2_send.at[n, o], red2_recv.at[n, lon], "lon",
                   lon_peer(o)).wait_send()

    def rec1(o, slot):
        return remote(rec_out1.at[lat_peer(o)], rec_in1.at[slot], rec1_send.at[o],
                      rec1_recv.at[slot], "lat", lat_peer(o))

    def rec2(o, slot):
        return remote(rec_out2.at[lon_peer(o)], rec_in2.at[slot], rec2_send.at[o],
                      rec2_recv.at[slot], "lon", lon_peer(o))

    d_load.wait()
    pack_lon(0, d_rows)
    pl.semaphore_wait(barrier, LAT + LON - 2)
    for copy in lon_copies(0):
        copy.start()

    @pl.loop(1, LAT)
    def _(o):
        rec1(o, lat).start()

    rec_in1[lat] = rec_out1[lat]
    own_part(0, d_rows)
    lon_part(0)

    @pl.loop(1, LAT)
    def _(o):
        rec1(o, lat_peer(o)).wait_recv()

    @pl.loop(0, LON // 2)
    def _(p):
        rows = pl.ds(p * 2 * CAP, 2 * CAP)
        for s in range(LAT // 2):
            first, second = rec_in1[2 * s, rows], rec_in1[2 * s + 1, rows]
            rec_out2[2 * p, 8 * s:8 * s + 8] = jnp.concatenate([first[:CAP], second[:CAP]], 0)
            rec_out2[2 * p + 1, 8 * s:8 * s + 8] = jnp.concatenate([first[CAP:], second[CAP:]], 0)

    @pl.loop(1, LON)
    def _(o):
        rec2(o, lon).start()

    rec_in2[lon] = rec_out2[lon]

    ens_load.wait()

    @pl.loop(0, LEV)
    def _(n):
        ens[pl.ds(n * 64, 64), :] = ens16[pl.ds(n * 64, 64), :].astype(F32)

    ens[8 * TILE:9 * TILE, :] = 0.5 * std_ref[...].astype(F32)

    r_load.wait()

    def squares(n, carry):
        total_r, total_d = carry
        value_r = r_nat[pl.ds(n * 40, 40), :]
        value_d = d_nat[pl.ds(n * 40, 40), :]
        for s in range(5):
            piece = value_r[s * 8:s * 8 + 8]
            total_r = total_r + piece * piece
            piece = value_d[s * 8:s * 8 + 8]
            total_d = total_d + piece * piece
        return total_r, total_d

    sum_r, sum_d = lax.fori_loop(0, LEV, squares, (zeros8, zeros8))

    @pl.loop(1, LON)
    def _(o):
        rec2(o, lon_peer(o)).wait_recv()

    records = rec_in2[...].reshape(LAT * LON * CAP, CELLS)
    high, low = split(records.T)
    rec_t[...] = jnp.concatenate([high, low], 0)
    cell = records[:, LEV:].astype(jnp.int32)

    @pl.loop(0, ROWS)
    def _(p):
        hit = cell == iota((LAT * LON * CAP, 2 * CELLS), 1) + p * 2 * CELLS
        both = mxu(rec_t[...], jnp.where(hit, 1.0, 0.0).astype(BF16))
        total = both[:CELLS] + both[CELLS:]
        dens[2 * p] = total[:, :CELLS]
        dens[2 * p + 1] = total[:, CELLS:]

    @pl.loop(0, 2 * ROWS)
    def _(q):
        inc[q] = jnp.zeros((CELLS, CELLS), F32)

    @pl.loop(0, MEMBERS)
    def _(k):
        lat_arrived(0, k)

        @pl.loop(0, CELLS // 8)
        def _(c):
            rows = lat_rows(0, k, c)
            for t in range(2):
                for i in range(ROWS):
                    inc[t * ROWS + i, pl.ds(c * 8, 8)] += ens_rows(2 * k + t, c, i) * rows[i]

    lat_arrived(0, MEMBERS)

    def adjoint(c, curve):
        rows = lat_rows(0, MEMBERS, c)
        part = pl.ds(c * 8, 8)
        for i in range(ROWS):
            spread = ens_rows(8, c, i)
            static = spread * rows[i]
            inc0 = inc[i, part] + static
            inc1 = inc[ROWS + i, part] + static
            back0 = dens[i, part] * inc0
            back1 = dens[ROWS + i, part] * inc1
            curve = curve + back0 * inc0 + back1 * inc1
            for m in range(MEMBERS):
                x_ref[m * ROWS + i, part] = (
                    ens_rows(2 * m, c, i) * back0 + ens_rows(2 * m + 1, c, i) * back1
                )
            x_ref[MEMBERS * ROWS + i, part] = spread * (back0 + back1)
        return curve

    curve = lax.fori_loop(0, CELLS // 8, adjoint, sum_d)
    lat_sent(0)
    pack_lon(1, x_rows)
    for copy in lon_copies(1):
        copy.start()
    reduce_first(0, 16, jnp.concatenate([sum_r, curve], 0))
    own_part(1, x_rows)
    reduce_second(0, 16)
    lon_part(1)
    sums = reduce_last(0, 16)
    norm_now = jnp.sum(sums[:8], keepdims=True)
    alpha = norm_now / jnp.sum(sums[8:], keepdims=True)

    def out_copy(k):
        rows = pl.ds(k * TILE, TILE)
        return pltpu.make_async_copy(o_nat.at[rows], out_hbm.at[rows], load_sem.at[3 + k])

    def update(k, total):
        lat_arrived(1, k)

        def body(c, total):
            rows = lat_rows(1, k, c)
            real = iota((8, CELLS), 0) + c * 8 < LEV
            for i in range(ROWS):
                at = pl.ds(k * TILE + c * 64 + i, 8, stride=ROWS)
                value = r_nat[at, :] - alpha * (d_nat[at, :] + rows[i])
                o_nat[at, :] = value
                value = jnp.where(real, value, 0.0)
                total = total + value * value
            return total

        total = lax.fori_loop(0, CELLS // 8, body, total)
        out_copy(k).start()
        return total

    total = lax.fori_loop(0, COMPS, update, zeros8)
    reduce_first(1, 8, total)
    reduce_second(1, 8)
    norm_next = jnp.sum(reduce_last(1, 8), keepdims=True)
    first = iota((8, CELLS), 0) == 0
    scalars_ref[...] = jnp.where(first, alpha, norm_next / norm_now)

    @pl.loop(0, COMPS)
    def _(k):
        out_copy(k).wait()

    lat_sent(1)
    for phase in range(2):
        for copy in lon_copies(phase):
            copy.wait_send()
    reduce_sent(0, 16)
    reduce_sent(1, 8)

    @pl.loop(1, LAT)
    def _(o):
        rec1(o, lat).wait_send()

    @pl.loop(1, LON)
    def _(o):
        rec2(o, lon).wait_send()


def on_device(
    control, residual, direction, ensemble, static_std, vertical, owner, column, slot, corner,
    obs_weight, live_count,
):
    flat = (COMPS * TILE, CELLS)
    vmem = pl.BlockSpec(memory_space=pltpu.VMEM)
    hbm = pl.BlockSpec(memory_space=pl.ANY)
    dma = pltpu.SemaphoreType.DMA
    tail = (COMPS * TILE + ROWS, CELLS)
    square = (CELLS, CELLS)
    new_residual, scalars = pl.pallas_call(
        kernel,
        out_shape=(
            jax.ShapeDtypeStruct(flat, F32),
            jax.ShapeDtypeStruct((8, CELLS), F32),
        ),
        in_specs=[pl.BlockSpec(memory_space=pltpu.SMEM)] + [vmem] * 7 + [hbm] * 3,
        out_specs=(hbm, vmem),
        scratch_shapes=[
            pltpu.VMEM(tail, F32),
            pltpu.VMEM(tail, F32),
            pltpu.VMEM(tail, F32),
            pltpu.VMEM((8 * TILE, CELLS), BF16),
            pltpu.VMEM((9 * TILE + ROWS, CELLS), F32),
            pltpu.VMEM((COMPS * ROWS,) + square, F32),
            pltpu.VMEM((COMPS * ROWS,) + square, F32),
            pltpu.VMEM((2 * COMPS, 2, 3) + square, F32),
            pltpu.VMEM((2, 2) + square, F32),
            pltpu.VMEM((2, 2) + square, F32),
            pltpu.VMEM((2,) + square, F32),
            pltpu.VMEM((2 * ROWS,) + square, F32),
            pltpu.VMEM((2 * ROWS,) + square, F32),
            pltpu.VMEM(square, F32),
            pltpu.VMEM((2, 2 * CELLS, 2 * CELLS), BF16),
            pltpu.VMEM((2, 2 * CELLS, 2 * CELLS), BF16),
            pltpu.VMEM((LAT, LON * CAP, CELLS), F32),
            pltpu.VMEM((LAT, LON * CAP, CELLS), F32),
            pltpu.VMEM((LON, LAT * CAP, CELLS), F32),
            pltpu.VMEM((LON, LAT * CAP, CELLS), F32),
            pltpu.VMEM((2 * CELLS, LAT * LON * CAP), BF16),
            pltpu.VMEM((2, LAT, 16, CELLS), F32),
            pltpu.VMEM((2, LON, 16, CELLS), F32),
            dma((8,)),
            dma((2, 2)), dma((2, 2)),
            dma((2 * COMPS, 2)), dma((2 * COMPS, 2)),
            dma((LAT,)), dma((LAT,)),
            dma((LON,)), dma((LON,)),
            dma((2, LAT)), dma((2, LAT)),
            dma((2, LON)), dma((2, LON)),
        ],
        compiler_params=pltpu.CompilerParams(
            collective_id=0, has_side_effects=True, vmem_limit_bytes=40 * 1024 * 1024
        ),
        name="analysis_step",
    )(
        live_count,
        owner.reshape(1, RECORDS),
        column.reshape(1, RECORDS),
        slot.reshape(1, RECORDS),
        corner.T,
        obs_weight,
        static_std.reshape(TILE, CELLS),
        vertical,
        direction.reshape(flat),
        residual.reshape(flat),
        ensemble.reshape(8 * TILE, CELLS),
    )
    alpha, beta = scalars[0, 0], scalars[1, 0]
    new_residual = new_residual.reshape(residual.shape)
    return control + alpha * direction, new_residual, new_residual + beta * direction


def solution(mesh):
    field = P(None, None, "lat", "lon")
    return jax.shard_map(
        on_device,
        mesh=mesh,
        in_specs=(
            field,
            field,
            field,
            P(None, None, None, "lat", "lon"),
            P(None, "lat", "lon"),
            P(),
            P(("lon", "lat"), None),
            P(("lon", "lat")),
            P(("lon", "lat")),
            P(("lon", "lat"), None),
            P(("lon", "lat"), None),
            P(("lon", "lat")),
        ),
        out_specs=(field, field, field),
        check_vma=False,
    )
```

time: 319 us -> 92.9 us (0.29)
  blocking collectives: 130 us -> 0 us
  Pallas kernels: 0 us -> 74.6 us
  local copies, waits for them, and re-layouts: 69 us -> 12.5 us
  starting transfers between devices: 45.1 us -> 0 us
  other arithmetic: 49 us -> 4.08 us
  matrix products: 14.4 us -> 0 us
  waiting for transfers between devices: 6.65 us -> 0 us
    psum x2 -> x0, blocking collectives: 130 us -> none  [the longest x1 65.7 us: on_device(): norm_now = lax.psum(jnp.sum(residual * residual), ('lon', 'lat'))]
    pallas_call x0 -> x1, Pallas kernels: none -> 74.6 us  [on_device(): pl.pallas_call(kernel, out_shape=(jax.ShapeDtypeStruct(flat, F32), jax.Sh...]
    unnamed x50 -> x23, local copies, waits for them, and re-layouts: 39.1 us -> 11.9 us
    ppermute x8 -> x0, starting transfers between devices: 25 us -> none  [the longest x4 13.7 us: extended_2(): before = lax.ppermute(last, axis, up)]
    add x4 -> x1, other arithmetic: 27 us -> 4.08 us  [on_device(): new_residual + beta * direction]
    all_to_all x2 -> x0, starting transfers between devices: 20.1 us -> none  [the longest x1 10.2 us: on_device(): lax.all_to_all(weight_buf.reshape(devices, capacity, levels), ('lon', 'la...]
    reduce_sum x5 -> x0, other arithmetic: 19.2 us -> none  [the longest x1 10.4 us: on_device(): curve = lax.psum(jnp.sum(direction * image), ('lon', 'lat'))]
    dot_general x4 -> x0, matrix products: 14.4 us -> none  [the longest x1 4.73 us: on_device(): jnp.einsum('tlc,rtc->rl', flat_inc, table, precision=lax.Precision.HIGHEST)]
  transfers between devices with their start and end apart: 10 -> 0, of which waited for: 3 -> 0; matrix products, arithmetic and copies ran while one was open for 14% -> 0% of each run, Pallas kernels for 0% -> 0%
where the time goes in v1:
time: 92.9 us; the launch traced here: 92.5 us
  Pallas kernels  74.6 us (80%)
  local copies, waits for them, and re-layouts  12.5 us (13%)
  other arithmetic  4.08 us (4%)
  between operations  1.31 us (1%)
    pallas_call x1, Pallas kernels, on_device(): pl.pallas_call(kernel, out_shape=(jax.ShapeDtypeStruct(flat, F32), jax.Sh...  74.6 us
    unnamed x23, local copies, waits for them, and re-layouts  11.9 us
    add x1, other arithmetic, on_device(): new_residual + beta * direction  4.08 us

profile of v1, /device:TPU:1, one launch (start us, length us, event | category | flops | bytes accessed | tf_op | source)
XLA Modules:
  0.0 92.5 jit_solution(17152780469921264430)
XLA Ops:
  1.3 0.0 copy-start
  1.3 1.7 %copy-done = f32[5,127,8,128]{3,2,1,0:T(8,128)S(1)} copy-done((f32[5,127,8,128]{3,2,1,0:T(8,128)S(1)}, f32[5,127,8,128]{3,2,1,0:T(8,128)}, u32[]{:S(2)}) %copy-start) | copy-done | bytes 2600984
  3.0 0.0 copy-start.1
  3.0 1.7 %copy-done.1 = f32[5,127,8,128]{3,2,1,0:T(8,128)S(1)} copy-done((f32[5,127,8,128]{3,2,1,0:T(8,128)S(1)}, f32[5,127,8,128]{3,2,1,0:T(8,128)}, u32[]{:S(2)}) %copy-start.1) | copy-done | bytes 2600984
  4.8 0.0 copy-start.2
  4.8 1.6 %copy-done.2 = bf16[4,2,127,8,128]{4,3,2,1,0:T(8,128)(2,1)S(1)} copy-done((bf16[4,2,127,8,128]{4,3,2,1,0:T(8,128)(2,1)S(1)}, bf16[4,2,127,8,128]{4,3,2,1,0:T(8,128)(2,1)}, u32[]{:S(2)}) %copy-start.2) | copy-done | bytes 2080792
  6.3 0.0 copy-start.3
  6.3 0.9 %copy-done.3 = bf16[127,8,128]{2,1,0:T(8,128)(2,1)S(1)} copy-done((bf16[127,8,128]{2,1,0:T(8,128)(2,1)S(1)}, bf16[127,8,128]{2,1,0:T(8,128)(2,1)}, u32[]{:S(2)}) %copy-start.3) | copy-done | bytes 260120
  7.3 0.0 copy-start.4
  7.3 0.9 copy-done.4
  8.2 0.0 copy-start.5
  8.2 0.8 copy-done.5
  9.0 0.0 copy-start.6
  9.0 0.7 copy-done.6
  9.7 0.0 copy-start.7
  9.7 0.7 copy-done.7
  10.4 0.0 copy-start.8
  10.4 0.7 copy-done.8
  11.1 0.0 copy-start.9
  11.1 0.7 copy-done.9
  11.8 0.0 copy-start.10
  11.8 74.6 %analysis_step.1 = (f32[5080,128]{1,0:T(8,128)S(1)}, f32[8,128]{1,0:T(8,128)S(1)}) custom-call(s32[1]{0:T(128)S(6)} %copy.16.live_ref, s32[1,256]{1,0:T(1,128)S(1)} %bitcast.18, s32[1,256]{1,0:T(1,128)S(1)} %bitcast.19, s32[1,256]{1,0:T(1,128)S(1)} %bitcast.20, s32[4,256]{1,0:T(4,128)S(1)} %bitcast.17, f32[256,127]{1,0:T(8,128)S(1)} %copy-done.4, ...), custom_call_target="tpu_custom_call" | custom-call | tf_op jit(solution)/shard_map/analysis_step/pallas_call | solution.py:527
  86.4 0.5 fusion
  86.9 0.0 copy-done.10
  86.9 4.1 %multiply_add_fusion = (f32[5,127,8,128]{3,2,1,0:T(8,128)}, f32[5,127,8,128]{3,2,1,0:T(8,128)}) fusion(f32[5,127,8,128]{3,2,1,0:T(8,128)S(1)} %bitcast.12, f32[5,127,8,128]{3,2,1,0:T(8,128)S(1)} %copy-done, f32[]{:T(128)} %bitcast.10, f32[5,127,8,128]{3,2,1,0:T(8,128)S(1)} %copy-done.10, f32[]{:T(128)} %bitcast.8), kind=kLoop, calls=%fused_computation | loop fusion | flops 2600960 | bytes 13004808 | tf_op jit(solution)/shard_map/add | solution.py:586
  91.0 1.5 %copy.17 = f32[5,127,8,128]{3,2,1,0:T(8,128)} copy(f32[5,127,8,128]{3,2,1,0:T(8,128)S(1)} %bitcast.13) | data formatting | bytes 5201920
Async XLA Ops:
  1.3 1.7 %copy-start = (f32[5,127,8,128]{3,2,1,0:T(8,128)S(1)}, f32[5,127,8,128]{3,2,1,0:T(8,128)}, u32[]{:S(2)}) copy-start(f32[5,127,8,128]{3,2,1,0:T(8,128)} %param.14) | copy-start | bytes 7802884
  3.0 1.7 %copy-start.1 = (f32[5,127,8,128]{3,2,1,0:T(8,128)S(1)}, f32[5,127,8,128]{3,2,1,0:T(8,128)}, u32[]{:S(2)}) copy-start(f32[5,127,8,128]{3,2,1,0:T(8,128)} %param.13) | copy-start | bytes 7802884
  4.8 1.6 %copy-start.2 = (bf16[4,2,127,8,128]{4,3,2,1,0:T(8,128)(2,1)S(1)}, bf16[4,2,127,8,128]{4,3,2,1,0:T(8,128)(2,1)}, u32[]{:S(2)}) copy-start(bf16[4,2,127,8,128]{4,3,2,1,0:T(8,128)(2,1)} %param.15) | copy-start | bytes 6242308
  6.3 0.9 %copy-start.3 = (bf16[127,8,128]{2,1,0:T(8,128)(2,1)S(1)}, bf16[127,8,128]{2,1,0:T(8,128)(2,1)}, u32[]{:S(2)}) copy-start(bf16[127,8,128]{2,1,0:T(8,128)(2,1)} %param.16) | copy-start | bytes 780292
  7.3 0.9 copy-start.4
  8.2 0.8 copy-start.5
  9.0 0.7 copy-start.6
  9.7 0.7 copy-start.7
  10.4 0.7 copy-start.8
  11.1 0.7 copy-start.9
  11.8 75.2 %copy-start.10 = (f32[5,127,8,128]{3,2,1,0:T(8,128)S(1)}, f32[5,127,8,128]{3,2,1,0:T(8,128)}, u32[]{:S(2)}) copy-start(f32[5,127,8,128]{3,2,1,0:T(8,128)} %param.12) | copy-start | bytes 7802884

commit v2 on v1

--- a/solution.py
+++ b/solution.py
@@ -17,6 +17,7 @@
 LON = 16
 RECORDS = 256
 CAP = 4
+PAIRS = COMPS * ROWS // 2
 F32 = jnp.float32
 BF16 = jnp.bfloat16
 
@@ -67,12 +68,14 @@
 
 
 def kernel(
-    live_ref, owner_ref, column_ref, slot_ref, corner_ref, weight_ref, std_ref, v_ref,
+    live_hbm, owner_hbm, column_hbm, slot_hbm, corner_hbm, weight_hbm, std_hbm, v_hbm,
     d_hbm, r_hbm, ens_hbm,
     out_hbm, scalars_ref,
-    d_nat, r_nat, o_nat, ens16, ens, x_ref, y_ref, halo, lon_out, lon_in, lon_lev, inc, dens,
-    vpad, level_w, lane_w, rec_out1, rec_in1, rec_out2, rec_in2, rec_t, part1, part2,
-    load_sem, lon_send, lon_recv, lat_send, lat_recv,
+    live_ref, owner_ref, column_ref, slot_ref, corner_ref, weight_ref, std_ref, v_ref,
+    d_nat, r_nat, o_nat, ens16, ens, x_ref, y_ref, halo, lon_out, lon_in, inc, dens,
+    vpad, level_w, lane_w, edge_w, pack_w, spread_w, rec_out1, rec_in1, rec_out2, rec_in2, rec_t,
+    part1, part2,
+    small_sem, load_sem, lon_send, lon_recv, lat_send, lat_recv,
     rec1_send, rec1_recv, rec2_send, rec2_recv, red1_send, red1_recv, red2_send, red2_recv,
 ):
     lon = lax.axis_index("lon")
@@ -111,6 +114,16 @@
     d_load = pltpu.make_async_copy(d_hbm, d_nat.at[pl.ds(0, COMPS * TILE)], load_sem.at[0])
     ens_load = pltpu.make_async_copy(ens_hbm, ens16, load_sem.at[1])
     r_load = pltpu.make_async_copy(r_hbm, r_nat.at[pl.ds(0, COMPS * TILE)], load_sem.at[2])
+    small_loads = [
+        pltpu.make_async_copy(src, dst, small_sem.at[n])
+        for n, (src, dst) in enumerate((
+            (live_hbm, live_ref), (owner_hbm, owner_ref), (column_hbm, column_ref),
+            (slot_hbm, slot_ref), (corner_hbm, corner_ref), (v_hbm, v_ref),
+            (weight_hbm, weight_ref), (std_hbm, std_ref),
+        ))
+    ]
+    for copy in small_loads:
+        copy.start()
     d_load.start()
     ens_load.start()
     r_load.start()
@@ -120,18 +133,47 @@
     r_nat[COMPS * TILE:, :] = zeros8
     ens[9 * TILE:, :] = zeros8
     vpad[...] = jnp.zeros((CELLS, CELLS), F32)
+
+    high_dim, low_dim = iota((2 * CELLS, 2 * CELLS), 0), iota((2 * CELLS, 2 * CELLS), 1)
+
+    def selection(cell, packed, first, last):
+        column, half = cell & (CELLS - 1), cell >> 7
+        where = jnp.where(
+            (column >= CELLS - 3) & (packed >= last) & (packed < last + CELLS),
+            packed - last - (column - (CELLS - 3)),
+            jnp.where(
+                (column < 3) & (packed >= first) & (packed < first + CELLS),
+                packed - first - column, -1000,
+            ),
+        )
+        return where - 3 * half
+
+    to_pack = selection(high_dim, low_dim, CELLS, 0)
+    to_cell = selection(low_dim, high_dim, 0, CELLS)
+
+    @pl.loop(0, PAIRS)
+    def _(p):
+        pack_w[p] = jnp.where(to_pack == 6 * p, 1.0, 0.0).astype(BF16)
+        spread_w[p] = jnp.where(to_cell == 6 * p, 1.0, 0.0).astype(BF16)
+
+    third = ((high_dim & (CELLS - 1)) * 43691) >> 17
+    same = (third == ((low_dim & (CELLS - 1)) * 43691) >> 17) & (high_dim >> 7 == low_dim >> 7)
+    step = jnp.where(high_dim < CELLS, high_dim - low_dim, low_dim - high_dim)
+    edge = jnp.zeros((2 * CELLS, 2 * CELLS), F32)
+    for k in range(1, 4):
+        edge = jnp.where(same & (step == 3 - k), taps[k], edge)
+    edge_w[0], edge_w[1] = split(edge)
+
+    for copy in small_loads:
+        copy.wait()
     vpad[0:LEV, 0:LEV] = v_ref[...]
     level_w[0] = level_matrix(vpad[...])
     level_w[1] = level_matrix(vpad[...].T)
     gap = jnp.abs(iota((CELLS, CELLS), 0) - lane)
     inner = jnp.zeros((CELLS, CELLS), F32)
-    wrapped = inner
     for k in range(4):
         inner = jnp.where(gap == k, taps[k], inner)
-        if k:
-            wrapped = jnp.where(gap == CELLS - k, taps[k], wrapped)
-    lane_w[0] = lane_matrix(inner)
-    lane_w[1] = lane_matrix(wrapped)
+    lane_w[...] = lane_matrix(inner)
 
     eye = iota((RECORDS, RECORDS), 0) == iota((RECORDS, RECORDS), 1)
     before = iota((RECORDS, RECORDS), 0) < iota((RECORDS, RECORDS), 1)
@@ -145,7 +187,7 @@
     )
     place_col = jnp.sum(jnp.where(eye, place, 0), axis=1, keepdims=True).astype(F32)
     target = (((owner & (LAT - 1)) * LON + (owner >> 3)) * CAP) + rank
-    target = jnp.where(iota((1, RECORDS), 1) < live_ref[0], target, -1)
+    target = jnp.where(iota((1, RECORDS), 1) < live_ref[...], target, -1)
     chosen = jnp.where(iota((LAT * LON * CAP, RECORDS), 0) == target, 1.0, 0.0).astype(BF16)
     weights = jnp.concatenate([weight_ref[...], place_col], 1)
     high = weights.astype(BF16)
@@ -169,25 +211,23 @@
         blank(1)
 
     def d_rows(q):
-        k, i = q // ROWS, lax.rem(q, ROWS)
+        k, i = q // ROWS, q % ROWS
         return d_nat[pl.ds(k * TILE + i, CELLS, stride=ROWS), :]
 
     def x_rows(q):
         return x_ref[q]
 
     def pack_lon(phase, rows):
-        def body(q, carry):
-            left, right = carry
-            value = rows(q)
-            here = (lane >= 3 * q) & (lane < 3 * q + 3)
-            left = jnp.where(here, pltpu.roll(value, 3 * q + 3, 1), left)
-            right = jnp.where(here, pltpu.roll(value, 3 * q, 1), right)
-            return left, right
-
-        zero = jnp.zeros((CELLS, CELLS), F32)
-        left, right = lax.fori_loop(0, COMPS * ROWS, body, (zero, zero))
-        lon_out[phase, 0] = left
-        lon_out[phase, 1] = right
+        total = None
+        for k in range(COMPS):
+            value = jnp.concatenate([rows(k * ROWS + i) for i in range(ROWS)], 1)
+            high, low = split(value)
+            weight = pack_w[4 * k:4 * k + 4].reshape(ROWS * CELLS, 2 * CELLS)
+            part = mxu(jnp.concatenate([high, low], 0), weight)
+            total = part if total is None else total + part
+        total = total[:CELLS] + total[CELLS:]
+        lon_out[phase, 0] = total[:, :CELLS]
+        lon_out[phase, 1] = total[:, CELLS:]
 
     def lon_copies(phase):
         return [
@@ -237,37 +277,31 @@
                 lat_south(phase, k).wait_send()
 
     def own_part(phase, rows):
-        @pl.loop(0, COMPS * ROWS // 2)
-        def _(p):
-            value = jnp.concatenate([rows(2 * p), rows(2 * p + 1)], 1)
+        for k in range(COMPS):
+            value = jnp.concatenate([rows(k * ROWS + i) for i in range(ROWS)], 1)
             value = level_product(level_w[phase], value)
-            value = jnp.concatenate([value[:, :CELLS], value[:, CELLS:]], 0)
-            value = lane_product(value, lane_w[0])
-            y_ref[2 * p] = value[:CELLS]
-            y_ref[2 * p + 1] = value[CELLS:]
+            value = jnp.concatenate(
+                [value[:, i * CELLS:(i + 1) * CELLS] for i in range(ROWS)], 0
+            )
+            value = lane_product(value, lane_w[...])
+            for i in range(ROWS):
+                y_ref[k * ROWS + i] = value[i * CELLS:(i + 1) * CELLS]
 
     def lon_part(phase):
         for copy in lon_copies(phase):
             copy.wait_recv()
         edges = jnp.concatenate([lon_in[phase, 0], lon_in[phase, 1]], 1)
-        edges = level_product(level_w[phase], edges)
-        lon_lev[0] = edges[:, :CELLS]
-        lon_lev[1] = edges[:, CELLS:]
-
-        def spread(q):
-            left = pltpu.roll(lon_lev[0], CELLS - 3 - 3 * q, 1)
-            right = pltpu.roll(lon_lev[1], lax.rem(CELLS - 3 * q, CELLS), 1)
-            return jnp.where(lane >= CELLS // 2, left, right)
-
-        @pl.loop(0, COMPS)
-        def _(k):
-            @pl.loop(0, ROWS // 2)
-            def _(p):
-                q = k * ROWS + 2 * p
-                value = lane_product(jnp.concatenate([spread(q), spread(q + 1)], 0), lane_w[1])
-                y_ref[q] += value[:CELLS]
-                y_ref[q + 1] += value[CELLS:]
-
+        high, low = split(level_product(level_w[phase], edges))
+        both = mxu(jnp.concatenate([high, low], 0), edge_w[0])
+        edges = both[:CELLS] + both[CELLS:] + mxu(high, edge_w[1])
+        high, low = split(edges)
+        edges = jnp.concatenate([high, low], 0)
+        for k in range(COMPS):
+            for p in range(4 * k, 4 * k + 4):
+                both = mxu(edges, spread_w[p])
+                both = both[:CELLS] + both[CELLS:]
+                y_ref[2 * p] += both[:, :CELLS]
+                y_ref[2 * p + 1] += both[:, CELLS:]
             lat_start(phase, k)
 
     def lat_rows(phase, k, c):
@@ -520,7 +554,7 @@
 ):
     flat = (COMPS * TILE, CELLS)
     vmem = pl.BlockSpec(memory_space=pltpu.VMEM)
-    hbm = pl.BlockSpec(memory_space=pl.ANY)
+    hbm = pl.BlockSpec(memory_space=pltpu.HBM)
     dma = pltpu.SemaphoreType.DMA
     tail = (COMPS * TILE + ROWS, CELLS)
     square = (CELLS, CELLS)
@@ -530,9 +564,17 @@
             jax.ShapeDtypeStruct(flat, F32),
             jax.ShapeDtypeStruct((8, CELLS), F32),
         ),
-        in_specs=[pl.BlockSpec(memory_space=pltpu.SMEM)] + [vmem] * 7 + [hbm] * 3,
+        in_specs=[hbm] * 11,
         out_specs=(hbm, vmem),
         scratch_shapes=[
+            pltpu.VMEM((1, 1), jnp.int32),
+            pltpu.VMEM((1, RECORDS), jnp.int32),
+            pltpu.VMEM((1, RECORDS), jnp.int32),
+            pltpu.VMEM((1, RECORDS), jnp.int32),
+            pltpu.VMEM((4, RECORDS), jnp.int32),
+            pltpu.VMEM((RECORDS, LEV), F32),
+            pltpu.VMEM((TILE, CELLS), BF16),
+            pltpu.VMEM((LEV, LEV), F32),
             pltpu.VMEM(tail, F32),
             pltpu.VMEM(tail, F32),
             pltpu.VMEM(tail, F32),
@@ -543,12 +585,14 @@
             pltpu.VMEM((2 * COMPS, 2, 3) + square, F32),
             pltpu.VMEM((2, 2) + square, F32),
             pltpu.VMEM((2, 2) + square, F32),
-            pltpu.VMEM((2,) + square, F32),
             pltpu.VMEM((2 * ROWS,) + square, F32),
             pltpu.VMEM((2 * ROWS,) + square, F32),
             pltpu.VMEM(square, F32),
             pltpu.VMEM((2, 2 * CELLS, 2 * CELLS), BF16),
+            pltpu.VMEM((2 * CELLS, 2 * CELLS), BF16),
             pltpu.VMEM((2, 2 * CELLS, 2 * CELLS), BF16),
+            pltpu.VMEM((PAIRS, 2 * CELLS, 2 * CELLS), BF16),
+            pltpu.VMEM((PAIRS, 2 * CELLS, 2 * CELLS), BF16),
             pltpu.VMEM((LAT, LON * CAP, CELLS), F32),
             pltpu.VMEM((LAT, LON * CAP, CELLS), F32),
             pltpu.VMEM((LON, LAT * CAP, CELLS), F32),
@@ -556,6 +600,7 @@
             pltpu.VMEM((2 * CELLS, LAT * LON * CAP), BF16),
             pltpu.VMEM((2, LAT, 16, CELLS), F32),
             pltpu.VMEM((2, LON, 16, CELLS), F32),
+            dma((8,)),
             dma((8,)),
             dma((2, 2)), dma((2, 2)),
             dma((2 * COMPS, 2)), dma((2 * COMPS, 2)),
@@ -565,11 +610,11 @@
             dma((2, LON)), dma((2, LON)),
         ],
         compiler_params=pltpu.CompilerParams(
-            collective_id=0, has_side_effects=True, vmem_limit_bytes=40 * 1024 * 1024
+            collective_id=0, has_side_effects=True, vmem_limit_bytes=60 * 1024 * 1024
         ),
         name="analysis_step",
     )(
-        live_count,
+        live_count.reshape(1, 1),
         owner.reshape(1, RECORDS),
         column.reshape(1, RECORDS),
         slot.reshape(1, RECORDS),

time: 92.9 us -> 72.4 us (0.78)
  Pallas kernels: 74.6 us -> 61.3 us
  local copies, waits for them, and re-layouts: 12.5 us -> 2.84 us
  other arithmetic: 4.08 us -> 6.77 us
    pallas_call x1, Pallas kernels: 74.6 us -> 61.3 us  [on_device(): pl.pallas_call(kernel, out_shape=(jax.ShapeDtypeStruct(flat, F32), jax.Sh...]
    unnamed x23 -> x5, local copies, waits for them, and re-layouts: 11.9 us -> 1.49 us
    add x1, other arithmetic: 4.08 us -> 6.77 us  [on_device(): new_residual + beta * direction]
where the time goes in v2:
time: 72.4 us; the launch traced here: 72.2 us
  Pallas kernels  61.3 us (85%)
  other arithmetic  6.77 us (9%)
  local copies, waits for them, and re-layouts  2.84 us (4%)
  between operations  1.3 us (2%)
    pallas_call x1, Pallas kernels, on_device(): pl.pallas_call(kernel, out_shape=(jax.ShapeDtypeStruct(flat, F32), jax.Sh...  61.3 us
    add x1, other arithmetic, on_device(): new_residual + beta * direction  6.77 us
    unnamed x5, local copies, waits for them, and re-layouts  1.49 us

profile of v2, /device:TPU:1, one launch (start us, length us, event | category | flops | bytes accessed | tf_op | source)
XLA Modules:
  0.0 72.2 jit_solution(3162322730458002067)
XLA Ops:
  1.3 0.0 copy-start
  1.3 61.3 %analysis_step.1 = (f32[5080,128]{1,0:T(8,128)}, f32[8,128]{1,0:T(8,128)}) custom-call(s32[1,1]{1,0:T(1,128)} %bitcast.12.live_hbm, s32[1,256]{1,0:T(1,128)} %bitcast.20, s32[1,256]{1,0:T(1,128)} %bitcast.21, s32[1,256]{1,0:T(1,128)} %bitcast.22, s32[4,256]{1,0:T(4,128)} %bitcast.19, f32[256,127]{1,0:T(8,128)} %weight_hbm.1, bf16[1016,128]{1,0:T(8,128)(2,1)} %bitcast.18, ...), custom_call_target="tpu_custom_call" | custom-call | tf_op jit(solution)/shard_map/analysis_step/pallas_call | solution.py:561
  62.6 1.3 %fusion = (f32[1,1]{1,0:T(1,128)}, f32[1,1]{1,0:T(1,128)}) fusion(f32[8,128]{1,0:T(8,128)} %get-tuple-element.5), kind=kLoop, calls=%fused_computation.2 | loop fusion | bytes 16 | tf_op jit(solution)/shard_map/slice | solution.py:629
  64.0 0.0 copy-done
  64.0 0.0 copy-start.1
  64.0 6.8 %multiply_add_fusion = (f32[5,127,8,128]{3,2,1,0:T(8,128)}, f32[5,127,8,128]{3,2,1,0:T(8,128)}) fusion(f32[5,127,8,128]{3,2,1,0:T(8,128)} %bitcast.14, f32[5,127,8,128]{3,2,1,0:T(8,128)S(1)} %copy-done, f32[]{:T(128)} %bitcast.11, f32[5,127,8,128]{3,2,1,0:T(8,128)} %param.12, f32[]{:T(128)} %bitcast.9), kind=kLoop, calls=%fused_computation | loop fusion | flops 2600960 | bytes 13004808 | tf_op jit(solution)/shard_map/add | solution.py:631
  70.8 0.0 copy-done.1
  70.8 1.5 %copy.17 = f32[5,127,8,128]{3,2,1,0:T(8,128)} copy(f32[5,127,8,128]{3,2,1,0:T(8,128)S(1)} %bitcast.15) | data formatting | bytes 5201920
Async XLA Ops:
  1.3 62.7 %copy-start = (f32[5,127,8,128]{3,2,1,0:T(8,128)S(1)}, f32[5,127,8,128]{3,2,1,0:T(8,128)}, u32[]{:S(2)}) copy-start(f32[5,127,8,128]{3,2,1,0:T(8,128)} %param.14) | copy-start | bytes 7802884
  64.0 6.8 %copy-start.1 = (f32[5080,128]{1,0:T(8,128)S(1)}, f32[5080,128]{1,0:T(8,128)}, u32[]{:S(2)}) copy-start(f32[5080,128]{1,0:T(8,128)} %get-tuple-element.6) | copy-start | bytes 7802884

commit v3 on v2

v3 whole, which is shorter than its diff:
```python
import math

import jax
import jax.numpy as jnp
from jax import lax
from jax.experimental import pallas as pl
from jax.experimental.pallas import tpu as pltpu
from jax.sharding import PartitionSpec as P

LEV = 127
COMPS = 5
MEMBERS = 4
ROWS = 8
CELLS = 128
TILE = LEV * ROWS
LAT = 8
LON = 16
RECORDS = 256
CAP = 4
PAIRS = COMPS * ROWS // 2
PACKED = [(q % COMPS) * ROWS + q // COMPS for q in range(COMPS * ROWS)]
EDGE = 3 * 3 * COMPS
F32 = jnp.float32
BF16 = jnp.bfloat16


def filter_taps():
    raw = [math.exp(-(offset * offset) / 8.0) for offset in range(-3, 4)]
    scale = math.sqrt(sum(value * value for value in raw))
    return [value / scale for value in raw[3:]]


def iota(shape, dim):
    return lax.broadcasted_iota(jnp.int32, shape, dim)


def split(value):
    high = value.astype(BF16)
    return high, (value - high.astype(F32)).astype(BF16)


def mxu(a, b):
    return lax.dot_general(a, b, (((1,), (0,)), ((), ())), preferred_element_type=F32)


def level_matrix(matrix):
    high, low = split(matrix)
    return jnp.concatenate(
        [jnp.concatenate([high, high], 1), jnp.concatenate([low, jnp.zeros_like(low)], 1)], 0
    )


def lane_matrix(matrix):
    high, low = split(matrix)
    return jnp.concatenate(
        [jnp.concatenate([high, low], 1), jnp.concatenate([high, jnp.zeros_like(low)], 1)], 0
    )


def level_product(matrix, field):
    high, low = split(field)
    both = mxu(matrix, jnp.concatenate([high, low], 0))
    return both[:CELLS] + both[CELLS:]


def lane_product(field, matrix):
    high, low = split(field)
    both = mxu(jnp.concatenate([high, low], 1), matrix)
    return both[:, :CELLS] + both[:, CELLS:]


def kernel(
    live_hbm, owner_hbm, column_hbm, slot_hbm, corner_hbm, weight_hbm, std_hbm, v_hbm,
    d_hbm, r_hbm, ens_hbm, c_hbm,
    control_ref, residual_ref, direction_ref,
    live_ref, owner_ref, column_ref, slot_ref, corner_ref, weight_ref, std_ref, v_ref,
    d_nat, r_nat, c_nat, ens16, ens, x_ref, y_ref, z_ref, halo, corner_rows, lon_out, lon_in,
    corner_out, corner_in, inc, dens,
    vpad, level_w, lane_w, edge_w, pack_w, spread_w, corner_w, rec_out1, rec_in1, rec_out2, rec_in2, rec_t,
    part1, part2,
    small_sem, d_sem, load_sem, lon_send, lon_recv, corner_send, corner_recv, lat_send, lat_recv,
    rec1_send, rec1_recv, rec2_send, rec2_recv, red1_send, red1_recv, red2_send, red2_recv,
):
    lon = lax.axis_index("lon")
    lat = lax.axis_index("lat")
    taps = filter_taps()
    lane = iota((CELLS, CELLS), 1)

    def lat_peer(o):
        return lax.rem(lat + o, LAT)

    def lon_peer(o):
        return lax.rem(lon + o, LON)

    east, west = lon_peer(1), lon_peer(LON - 1)

    def remote(src, dst, send, recv, axis, peer):
        return pltpu.make_async_remote_copy(
            src_ref=src, dst_ref=dst, send_sem=send, recv_sem=recv,
            device_id={axis: peer}, device_id_type=pl.DeviceIdType.MESH,
        )

    barrier = pltpu.get_barrier_semaphore()

    @pl.loop(1, LAT)
    def _(o):
        pl.semaphore_signal(
            barrier, inc=1, device_id={"lat": lat_peer(o)}, device_id_type=pl.DeviceIdType.MESH
        )

    @pl.loop(1, LON)
    def _(o):
        pl.semaphore_signal(
            barrier, inc=1, device_id={"lon": lon_peer(o)}, device_id_type=pl.DeviceIdType.MESH
        )

    d_loads = [
        pltpu.make_async_copy(
            d_hbm.at[pl.ds(k * TILE, TILE)], d_nat.at[pl.ds(k * TILE, TILE)], d_sem.at[k]
        )
        for k in range(COMPS)
    ]
    ens_load = pltpu.make_async_copy(ens_hbm, ens16, load_sem.at[0])
    r_load = pltpu.make_async_copy(r_hbm, r_nat.at[pl.ds(0, COMPS * TILE)], load_sem.at[1])
    c_load = pltpu.make_async_copy(c_hbm, c_nat, load_sem.at[2])
    small_loads = [
        pltpu.make_async_copy(src, dst, small_sem.at[n])
        for n, (src, dst) in enumerate((
            (live_hbm, live_ref), (owner_hbm, owner_ref), (column_hbm, column_ref),
            (slot_hbm, slot_ref), (corner_hbm, corner_ref), (v_hbm, v_ref),
            (weight_hbm, weight_ref), (std_hbm, std_ref),
        ))
    ]
    small_loads[5].start()
    for copy in d_loads:
        copy.start()
    for n, copy in enumerate(small_loads):
        if n != 5:
            copy.start()
    ens_load.start()
    r_load.start()
    c_load.start()

    zeros8 = jnp.zeros((ROWS, CELLS), F32)
    d_nat[COMPS * TILE:, :] = zeros8
    r_nat[COMPS * TILE:, :] = zeros8
    ens[9 * TILE:, :] = zeros8
    vpad[...] = jnp.zeros((CELLS, CELLS), F32)

    small_loads[5].wait()
    vpad[0:LEV, 0:LEV] = v_ref[...]
    level_w[0] = level_matrix(vpad[...])
    level_w[1] = level_matrix(vpad[...].T)
    gap = jnp.abs(iota((CELLS, CELLS), 0) - lane)
    inner = jnp.zeros((CELLS, CELLS), F32)
    for k in range(4):
        inner = jnp.where(gap == k, taps[k], inner)
    lane_w[...] = lane_matrix(inner)

    def build_selections():
        part = iota((2 * CELLS, 2 * CELLS), 0) & (CELLS - 1)
        cells = iota((2 * CELLS, 2 * CELLS), 1)
        column = cells & (CELLS - 1)
        wanted = jnp.where(
            (column < 3) & (part < CELLS // 2), part - column,
            jnp.where(
                (column >= CELLS - 3) & (part >= CELLS // 2),
                part - CELLS // 2 - (column - (CELLS - 3)), -1000,
            ),
        ) - 3 * (cells >> 7)

        @pl.loop(0, 8)
        def _(p):
            corner_w[p] = jnp.where(wanted == 6 * p, 1.0, 0.0).astype(BF16)

        high_dim, low_dim = iota((2 * CELLS, 2 * CELLS), 0), iota((2 * CELLS, 2 * CELLS), 1)

        def selection(cell, packed, first, last):
            column, half = cell & (CELLS - 1), cell >> 7
            where = jnp.where(
                (column >= CELLS - 3) & (packed >= last) & (packed < last + CELLS),
                packed - last - (column - (CELLS - 3)),
                jnp.where(
                    (column < 3) & (packed >= first) & (packed < first + CELLS),
                    packed - first - column, -1000,
                ),
            )
            return where - 3 * half

        to_pack = selection(high_dim, low_dim, CELLS, 0)
        to_cell = selection(low_dim, high_dim, 0, CELLS)

        @pl.loop(0, PAIRS)
        def _(p):
            pack_w[p] = jnp.where(to_pack == 6 * p, 1.0, 0.0).astype(BF16)
            spread_w[p] = jnp.where(to_cell == 6 * p, 1.0, 0.0).astype(BF16)

        third = ((high_dim & (CELLS - 1)) * 43691) >> 17
        same = (third == ((low_dim & (CELLS - 1)) * 43691) >> 17) & (high_dim >> 7 == low_dim >> 7)
        step = jnp.where(high_dim < CELLS, high_dim - low_dim, low_dim - high_dim)
        edge = jnp.zeros((2 * CELLS, 2 * CELLS), F32)
        for k in range(1, 4):
            edge = jnp.where(same & (step == 3 - k), taps[k], edge)
        edge_w[0], edge_w[1] = split(edge)

    def pack_records():
        for n, copy in enumerate(small_loads):
            if n != 5:
                copy.wait()
        eye = iota((RECORDS, RECORDS), 0) == iota((RECORDS, RECORDS), 1)
        before = iota((RECORDS, RECORDS), 0) < iota((RECORDS, RECORDS), 1)
        owner = owner_ref[...]
        owner_col = jnp.sum(jnp.where(eye, owner, 0), axis=1, keepdims=True)
        rank = jnp.sum(jnp.where((owner_col == owner) & before, 1, 0), axis=0, keepdims=True)
        corner = corner_ref[...]
        place = (
            slot_ref[...] * (ROWS * CELLS) + column_ref[...]
            + corner[1:2] + CELLS * corner[2:3] + (CELLS + 1) * corner[3:4]
        )
        place_col = jnp.sum(jnp.where(eye, place, 0), axis=1, keepdims=True).astype(F32)
        target = (((owner & (LAT - 1)) * LON + (owner >> 3)) * CAP) + rank
        target = jnp.where(iota((1, RECORDS), 1) < live_ref[...], target, -1)
        chosen = jnp.where(iota((LAT * LON * CAP, RECORDS), 0) == target, 1.0, 0.0).astype(BF16)
        weights = jnp.concatenate([weight_ref[...], place_col], 1)
        high = weights.astype(BF16)
        mid = (weights - high.astype(F32)).astype(BF16)
        packed = mxu(chosen, jnp.concatenate([high, mid], 1))
        packed = packed[:, :CELLS] + packed[:, CELLS:]
        for s in range(LAT):
            rec_out1[s] = packed[s * LON * CAP:(s + 1) * LON * CAP]

    def blank(side):
        @pl.loop(0, 2 * COMPS)
        def _(n):
            halo[n, side] = jnp.zeros((3, CELLS, CELLS), F32)

        @pl.loop(0, COMPS)
        def _(k):
            corner_rows[k, side] = jnp.zeros((3, CELLS, CELLS), F32)

    @pl.when(lat == 0)
    def _():
        blank(0)

    @pl.when(lat == LAT - 1)
    def _():
        blank(1)

    def d_rows(q):
        k, i = q // ROWS, q % ROWS
        return d_nat[pl.ds(k * TILE + i, CELLS, stride=ROWS), :]

    def x_rows(q):
        return x_ref[q]

    def pack_lon(phase, rows):
        total = None
        for k in range(COMPS):
            value = jnp.concatenate([rows(PACKED[k * ROWS + i]) for i in range(ROWS)], 1)
            high, low = split(value)
            weight = pack_w[4 * k:4 * k + 4].reshape(ROWS * CELLS, 2 * CELLS)
            part = mxu(jnp.concatenate([high, low], 0), weight)
            total = part if total is None else total + part
        total = total[:CELLS] + total[CELLS:]
        lon_out[phase, 0] = total[:, :CELLS]
        lon_out[phase, 1] = total[:, CELLS:]

    def edge_copies(phase):
        return [
            remote(lon_out.at[phase, side], lon_in.at[phase, side], lon_send.at[phase, side],
                   lon_recv.at[phase, side], "lon", (east, west)[side])
            for side in range(2)
        ]

    def corner_north(phase):
        return remote(corner_out.at[phase, 0], corner_in.at[phase, 1], corner_send.at[phase, 1],
                      corner_recv.at[phase, 1], "lat", lax.rem(lat + LAT - 1, LAT))

    def corner_south(phase):
        return remote(corner_out.at[phase, 1], corner_in.at[phase, 0], corner_send.at[phase, 0],
                      corner_recv.at[phase, 0], "lat", lax.rem(lat + 1, LAT))

    def lat_north(phase, k):
        n = phase * COMPS + k
        return remote(y_ref.at[pl.ds(k * ROWS, 3)], halo.at[n, 1], lat_send.at[n, 1],
                      lat_recv.at[n, 1], "lat", lax.rem(lat + LAT - 1, LAT))

    def lat_south(phase, k):
        n = phase * COMPS + k
        return remote(y_ref.at[pl.ds(k * ROWS + 5, 3)], halo.at[n, 0], lat_send.at[n, 0],
                      lat_recv.at[n, 0], "lat", lax.rem(lat + 1, LAT))

    def lat_start(phase, k):
        @pl.when(lat > 0)
        def _():
            lat_north(phase, k).start()

        @pl.when(lat < LAT - 1)
        def _():
            lat_south(phase, k).start()

    def lat_arrived(phase, k):
        @pl.when(lat > 0)
        def _():
            lat_south(phase, k).wait_recv()

        @pl.when(lat < LAT - 1)
        def _():
            lat_north(phase, k).wait_recv()

    def lat_sent(phase):
        @pl.loop(0, COMPS)
        def _(k):
            @pl.when(lat > 0)
            def _():
                lat_north(phase, k).wait_send()

            @pl.when(lat < LAT - 1)
            def _():
                lat_south(phase, k).wait_send()

    def own_part(phase, k, rows):
        value = jnp.concatenate([rows(k * ROWS + i) for i in range(ROWS)], 1)
        value = level_product(level_w[phase], value)
        value = jnp.concatenate([value[:, i * CELLS:(i + 1) * CELLS] for i in range(ROWS)], 0)
        value = lane_product(value, lane_w[...])
        for i in range(ROWS):
            y_ref[k * ROWS + i] = value[i * CELLS:(i + 1) * CELLS]

    def lon_part(phase):
        for copy in edge_copies(phase):
            copy.wait_recv()
        edges = jnp.concatenate([lon_in[phase, 0], lon_in[phase, 1]], 1)
        high, low = split(level_product(level_w[phase], edges))
        both = mxu(jnp.concatenate([high, low], 0), edge_w[0])
        edges = both[:CELLS] + both[CELLS:] + mxu(high, edge_w[1])
        left, right = edges[:, :CELLS], edges[:, CELLS:]
        half = CELLS // 2
        corner_out[phase, 0] = jnp.where(lane < half, left, pltpu.roll(right, half, 1))
        start = COMPS * ROWS * 3 - EDGE
        corner_out[phase, 1] = jnp.where(
            lane < half, pltpu.roll(left, CELLS - start, 1),
            pltpu.roll(right, CELLS + half - start, 1),
        )

        @pl.when(lat > 0)
        def _():
            corner_north(phase).start()

        @pl.when(lat < LAT - 1)
        def _():
            corner_south(phase).start()

        high, low = split(edges)
        edges = jnp.concatenate([high, low], 0)
        for p in range(PAIRS):
            both = mxu(edges, spread_w[p])
            both = both[:CELLS] + both[CELLS:]
            for n in range(2):
                q = PACKED[2 * p + n]
                z_ref[q] = y_ref[q] + both[:, n * CELLS:(n + 1) * CELLS]

    def corner_part(phase):
        def fill(side):
            high, low = split(corner_in[phase, side])
            edges = jnp.concatenate([high, low], 1)
            for p in range(8):
                both = mxu(edges, corner_w[p])
                for n in range(2):
                    q = 2 * p + n
                    if q < 3 * COMPS:
                        corner_rows[q % COMPS, side, q // COMPS] = (
                            both[:, n * CELLS:(n + 1) * CELLS]
                        )

        @pl.when(lat > 0)
        def _():
            corner_south(phase).wait_recv()
            fill(0)

        @pl.when(lat < LAT - 1)
        def _():
            corner_north(phase).wait_recv()
            fill(1)

    def lat_rows(phase, k, c):
        part = pl.ds(c * 8, 8)
        n = phase * COMPS + k
        rows = [halo[n, 0, j, part] + corner_rows[k, 0, j, part] for j in range(3)]
        rows += [z_ref[k * ROWS + i, part] for i in range(ROWS)]
        rows += [halo[n, 1, j, part] + corner_rows[k, 1, j, part] for j in range(3)]
        out = []
        for i in range(ROWS):
            total = taps[0] * rows[i + 3]
            for j in range(1, 4):
                total = total + taps[j] * (rows[i + 3 - j] + rows[i + 3 + j])
            out.append(total)
        return out

    def ens_rows(plane, c, i):
        return ens[pl.ds(plane * TILE + c * 64 + i, 8, stride=ROWS), :]

    def reduce_first(n, value):
        part1[n, lat] = value

        @pl.loop(1, LAT)
        def _(o):
            ref = part1.at[n, lat]
            remote(ref, ref, red1_send.at[n], red1_recv.at[n], "lat", lat_peer(o)).start()

    def first_all(n):
        ref = part1.at[n, pl.ds(0, LAT - 1)]
        return remote(ref, ref, red1_send.at[n], red1_recv.at[n], "lat", lat_peer(1))

    def second_all(n):
        ref = part2.at[n, pl.ds(0, LON - 1)]
        return remote(ref, ref, red2_send.at[n], red2_recv.at[n], "lon", lon_peer(1))

    def reduce_second(n):
        first_all(n).wait_recv()
        total = part1[n, 0]
        for s in range(1, LAT):
            total = total + part1[n, s]
        part2[n, lon] = total

        @pl.loop(1, LON)
        def _(o):
            ref = part2.at[n, lon]
            remote(ref, ref, red2_send.at[n], red2_recv.at[n], "lon", lon_peer(o)).start()

    def reduce_last(n):
        second_all(n).wait_recv()
        total = part2[n, 0]
        for s in range(1, LON):
            total = total + part2[n, s]
        return total

    def rec1(o):
        return remote(rec_out1.at[lat_peer(o)], rec_in1.at[lat], rec1_send.at[0],
                      rec1_recv.at[0], "lat", lat_peer(o))

    def rec2(o):
        return remote(rec_out2.at[lon_peer(o)], rec_in2.at[lon], rec2_send.at[0],
                      rec2_recv.at[0], "lon", lon_peer(o))

    def rec1_all():
        return remote(rec_out1.at[pl.ds(0, LAT - 1)], rec_in1.at[pl.ds(0, LAT - 1)],
                      rec1_send.at[0], rec1_recv.at[0], "lat", lat_peer(1))

    def rec2_all():
        return remote(rec_out2.at[pl.ds(0, LON - 1)], rec_in2.at[pl.ds(0, LON - 1)],
                      rec2_send.at[0], rec2_recv.at[0], "lon", lon_peer(1))

    d_loads[0].wait()
    d_loads[1].wait()
    own_part(0, 0, d_rows)
    build_selections()
    pl.semaphore_wait(barrier, LAT + LON - 2)
    lat_start(0, 0)
    pack_records()

    @pl.loop(1, LAT)
    def _(o):
        rec1(o).start()

    rec_in1[lat] = rec_out1[lat]
    for copy in d_loads[2:]:
        copy.wait()
    own_part(0, 1, d_rows)
    lat_start(0, 1)
    pack_lon(0, d_rows)
    for copy in edge_copies(0):
        copy.start()
    for k in range(2, COMPS):
        own_part(0, k, d_rows)
        lat_start(0, k)

    rec1_all().wait_recv()

    @pl.loop(0, LON // 2)
    def _(p):
        rows = pl.ds(p * 2 * CAP, 2 * CAP)
        for s in range(LAT // 2):
            first, second = rec_in1[2 * s, rows], rec_in1[2 * s + 1, rows]
            rec_out2[2 * p, 8 * s:8 * s + 8] = jnp.concatenate([first[:CAP], second[:CAP]], 0)
            rec_out2[2 * p + 1, 8 * s:8 * s + 8] = jnp.concatenate([first[CAP:], second[CAP:]], 0)

    @pl.loop(1, LON)
    def _(o):
        rec2(o).start()

    rec_in2[lon] = rec_out2[lon]
    lon_part(0)
    ens_load.wait()

    @pl.loop(0, LEV)
    def _(n):
        ens[pl.ds(n * 64, 64), :] = ens16[pl.ds(n * 64, 64), :].astype(F32)

    ens[8 * TILE:9 * TILE, :] = 0.5 * std_ref[...].astype(F32)

    r_load.wait()

    def squares(n, carry):
        total_r, total_d = carry
        value_r = r_nat[pl.ds(n * 40, 40), :]
        value_d = d_nat[pl.ds(n * 40, 40), :]
        for s in range(5):
            piece = value_r[s * 8:s * 8 + 8]
            total_r = total_r + piece * piece
            piece = value_d[s * 8:s * 8 + 8]
            total_d = total_d + piece * piece
        return total_r, total_d

    sum_r, sum_d = lax.fori_loop(0, LEV, squares, (zeros8, zeros8))
    rec2_all().wait_recv()

    records = rec_in2[...].reshape(LAT * LON * CAP, CELLS)
    high, low = split(records.T)
    rec_t[...] = jnp.concatenate([high, low], 0)
    cell = records[:, LEV:].astype(jnp.int32)

    @pl.loop(0, ROWS)
    def _(p):
        hit = cell == iota((LAT * LON * CAP, 2 * CELLS), 1) + p * 2 * CELLS
        both = mxu(rec_t[...], jnp.where(hit, 1.0, 0.0).astype(BF16))
        total = both[:CELLS] + both[CELLS:]
        dens[2 * p] = total[:, :CELLS]
        dens[2 * p + 1] = total[:, CELLS:]

    @pl.loop(0, 2 * ROWS)
    def _(q):
        inc[q] = jnp.zeros((CELLS, CELLS), F32)

    corner_part(0)

    @pl.loop(0, MEMBERS)
    def _(k):
        lat_arrived(0, k)

        @pl.loop(0, CELLS // 8)
        def _(c):
            rows = lat_rows(0, k, c)
            for t in range(2):
                for i in range(ROWS):
                    inc[t * ROWS + i, pl.ds(c * 8, 8)] += ens_rows(2 * k + t, c, i) * rows[i]

    lat_arrived(0, MEMBERS)

    def adjoint(c, curve):
        rows = lat_rows(0, MEMBERS, c)
        part = pl.ds(c * 8, 8)
        for i in range(ROWS):
            spread = ens_rows(8, c, i)
            static = spread * rows[i]
            inc0 = inc[i, part] + static
            inc1 = inc[ROWS + i, part] + static
            back0 = dens[i, part] * inc0
            back1 = dens[ROWS + i, part] * inc1
            curve = curve + back0 * inc0 + back1 * inc1
            for m in range(MEMBERS):
                x_ref[m * ROWS + i, part] = (
                    ens_rows(2 * m, c, i) * back0 + ens_rows(2 * m + 1, c, i) * back1
                )
            x_ref[MEMBERS * ROWS + i, part] = spread * (back0 + back1)
        return curve

    curve = lax.fori_loop(0, CELLS // 8, adjoint, sum_d)
    lat_sent(0)
    for k in range(COMPS):
        own_part(1, k, x_rows)
        lat_start(1, k)
        if k == 0:
            pack_lon(1, x_rows)
            for copy in edge_copies(1):
                copy.start()
        if k == 1:
            sums = jnp.where(
                iota((8, CELLS), 0) == 0, jnp.sum(sum_r, axis=0, keepdims=True),
                jnp.where(
                    iota((8, CELLS), 0) == 1, jnp.sum(curve, axis=0, keepdims=True), 0.0
                ),
            )
            reduce_first(0, sums)
    reduce_second(0)
    lon_part(1)
    sums = reduce_last(0)
    norm_now = jnp.sum(sums[0:1], keepdims=True)
    alpha = norm_now / jnp.sum(sums[1:2], keepdims=True)

    c_load.wait()

    @pl.loop(0, LEV)
    def _(n):
        part = pl.ds(n * 40, 40)
        control_ref[part, :] = c_nat[part, :] + alpha * d_nat[part, :]

    corner_part(1)

    def update(k, total):
        lat_arrived(1, k)

        def body(c, total, height=8):
            rows = lat_rows(1, k, c)
            for i in range(ROWS):
                at = pl.ds(k * TILE + c * 64 + i, height, stride=ROWS)
                value = r_nat[at, :] - alpha * (d_nat[at, :] + rows[i][:height])
                residual_ref[at, :] = value
                total[height] = total[height] + value * value
            return total

        total = lax.fori_loop(0, LEV // 8, body, total)
        return body(LEV // 8, total, LEV % 8)

    def finish(n, carry):
        part = pl.ds(n * 40, 40)
        direction_ref[part, :] = residual_ref[part, :] + beta * d_nat[part, :]
        return carry

    total = lax.fori_loop(0, COMPS, update, {8: zeros8, 7: zeros8[:7]})
    last = jnp.concatenate([total[7], jnp.zeros((1, CELLS), F32)], 0)
    reduce_first(1, total[8] + last)
    reduce_second(1)
    norm_next = jnp.sum(reduce_last(1), keepdims=True)
    beta = norm_next / norm_now
    lax.fori_loop(0, LEV, finish, 0)

    lat_sent(1)
    for phase in range(2):
        for copy in edge_copies(phase):
            copy.wait_send()

        @pl.when(lat > 0)
        def _():
            corner_north(phase).wait_send()

        @pl.when(lat < LAT - 1)
        def _():
            corner_south(phase).wait_send()

        first_all(phase).wait_send()
        second_all(phase).wait_send()
    rec1_all().wait_send()
    rec2_all().wait_send()


def on_device(
    control, residual, direction, ensemble, static_std, vertical, owner, column, slot, corner,
    obs_weight, live_count,
):
    flat = (COMPS * TILE, CELLS)
    vmem = pl.BlockSpec(memory_space=pltpu.VMEM)
    hbm = pl.BlockSpec(memory_space=pltpu.HBM)
    dma = pltpu.SemaphoreType.DMA
    tail = (COMPS * TILE + ROWS, CELLS)
    square = (CELLS, CELLS)
    results = pl.pallas_call(
        kernel,
        out_shape=(pltpu.VMEM(flat, F32),) * 3,
        in_specs=[hbm] * 12,
        out_specs=(vmem,) * 3,
        scratch_shapes=[
            pltpu.VMEM((1, 1), jnp.int32),
            pltpu.VMEM((1, RECORDS), jnp.int32),
            pltpu.VMEM((1, RECORDS), jnp.int32),
            pltpu.VMEM((1, RECORDS), jnp.int32),
            pltpu.VMEM((4, RECORDS), jnp.int32),
            pltpu.VMEM((RECORDS, LEV), F32),
            pltpu.VMEM((TILE, CELLS), BF16),
            pltpu.VMEM((LEV, LEV), F32),
            pltpu.VMEM(tail, F32),
            pltpu.VMEM(tail, F32),
            pltpu.VMEM(flat, F32),
            pltpu.VMEM((8 * TILE, CELLS), BF16),
            pltpu.VMEM((9 * TILE + ROWS, CELLS), F32),
            pltpu.VMEM((COMPS * ROWS,) + square, F32),
            pltpu.VMEM((COMPS * ROWS,) + square, F32),
            pltpu.VMEM((COMPS * ROWS,) + square, F32),
            pltpu.VMEM((2 * COMPS, 2, 3) + square, F32),
            pltpu.VMEM((COMPS, 2, 3) + square, F32),
            pltpu.VMEM((2, 2) + square, F32),
            pltpu.VMEM((2, 2) + square, F32),
            pltpu.VMEM((2, 2) + square, F32),
            pltpu.VMEM((2, 2) + square, F32),
            pltpu.VMEM((2 * ROWS,) + square, F32),
            pltpu.VMEM((2 * ROWS,) + square, F32),
            pltpu.VMEM(square, F32),
            pltpu.VMEM((2, 2 * CELLS, 2 * CELLS), BF16),
            pltpu.VMEM((2 * CELLS, 2 * CELLS), BF16),
            pltpu.VMEM((2, 2 * CELLS, 2 * CELLS), BF16),
            pltpu.VMEM((PAIRS, 2 * CELLS, 2 * CELLS), BF16),
            pltpu.VMEM((PAIRS, 2 * CELLS, 2 * CELLS), BF16),
            pltpu.VMEM((8, 2 * CELLS, 2 * CELLS), BF16),
            pltpu.VMEM((LAT, LON * CAP, CELLS), F32),
            pltpu.VMEM((LAT, LON * CAP, CELLS), F32),
            pltpu.VMEM((LON, LAT * CAP, CELLS), F32),
            pltpu.VMEM((LON, LAT * CAP, CELLS), F32),
            pltpu.VMEM((2 * CELLS, LAT * LON * CAP), BF16),
            pltpu.VMEM((2, LAT, 8, CELLS), F32),
            pltpu.VMEM((2, LON, 8, CELLS), F32),
            dma((8,)),
            dma((COMPS,)),
            dma((3,)),
            dma((2, 2)), dma((2, 2)),
            dma((2, 2)), dma((2, 2)),
            dma((2 * COMPS, 2)), dma((2 * COMPS, 2)),
            dma((1,)), dma((1,)),
            dma((1,)), dma((1,)),
            dma((2,)), dma((2,)),
            dma((2,)), dma((2,)),
        ],
        compiler_params=pltpu.CompilerParams(
            collective_id=0, has_side_effects=True, vmem_limit_bytes=55 * 1024 * 1024
        ),
        name="analysis_step",
    )(
        live_count.reshape(1, 1),
        owner.reshape(1, RECORDS),
        column.reshape(1, RECORDS),
        slot.reshape(1, RECORDS),
        corner.T,
        obs_weight,
        static_std.reshape(TILE, CELLS),
        vertical,
        direction.reshape(flat),
        residual.reshape(flat),
        ensemble.reshape(8 * TILE, CELLS),
        control.reshape(flat),
    )
    return tuple(result.reshape(control.shape) for result in results)


def solution(mesh):
    field = P(None, None, "lat", "lon")
    return jax.shard_map(
        on_device,
        mesh=mesh,
        in_specs=(
            field,
            field,
            field,
            P(None, None, None, "lat", "lon"),
            P(None, "lat", "lon"),
            P(),
            P(("lon", "lat"), None),
            P(("lon", "lat")),
            P(("lon", "lat")),
            P(("lon", "lat"), None),
            P(("lon", "lat"), None),
            P(("lon", "lat")),
        ),
        out_specs=(field, field, field),
        check_vma=False,
    )
```

time: 72.4 us -> 63.1 us (0.87)
  other arithmetic: 6.77 us -> 0 us
  Pallas kernels: 61.3 us -> 57.3 us
  local copies, waits for them, and re-layouts: 2.84 us -> 4.46 us
    add x1 -> x0, other arithmetic: 6.77 us -> none  [on_device(): new_residual + beta * direction]
    pallas_call x1, Pallas kernels: 61.3 us -> 57.3 us  [on_device(): pl.pallas_call(kernel, out_shape=(pltpu.VMEM(flat, F32),) * 3, in_specs=[...]
    unnamed x5 -> x3, local copies, waits for them, and re-layouts: 1.49 us -> 4.46 us
    slice x1 -> x0, local copies, waits for them, and re-layouts: 1.34 us -> none  [on_device(): alpha, beta = (scalars[0, 0], scalars[1, 0])]
where the time goes in v3:
time: 63.1 us; the launch traced here: 63 us
  Pallas kernels  57.3 us (91%)
  local copies, waits for them, and re-layouts  4.46 us (7%)
  between operations  1.29 us (2%)
    pallas_call x1, Pallas kernels, on_device(): pl.pallas_call(kernel, out_shape=(pltpu.VMEM(flat, F32),) * 3, in_specs=[...  57.3 us
    unnamed x3, local copies, waits for them, and re-layouts  4.46 us

profile of v3, /device:TPU:1, one launch (start us, length us, event | category | flops | bytes accessed | tf_op | source)
XLA Modules:
  0.0 63.0 jit_solution(15610878746270072920)
XLA Ops:
  1.3 57.3 %analysis_step.1 = (f32[5080,128]{1,0:T(8,128)S(1)}, f32[5080,128]{1,0:T(8,128)S(1)}, f32[5080,128]{1,0:T(8,128)S(1)}) custom-call(s32[1,1]{1,0:T(1,128)} %bitcast.13.live_hbm, s32[1,256]{1,0:T(1,128)} %bitcast.23, s32[1,256]{1,0:T(1,128)} %bitcast.24, s32[1,256]{1,0:T(1,128)} %bitcast.25, s32[4,256]{1,0:T(4,128)} %bitcast.22, f32[256,127]{1,0:T(8,128)} %weight_hbm.1, ...), custom_call_target="tpu_custom_call" | custom-call | tf_op jit(solution)/shard_map/analysis_step/pallas_call | solution.py:657
  58.6 1.5 %copy.18 = f32[5,127,8,128]{3,2,1,0:T(8,128)} copy(f32[5,127,8,128]{3,2,1,0:T(8,128)S(1)} %bitcast.16) | data formatting | bytes 5201920
  60.1 1.5 %copy.19 = f32[5,127,8,128]{3,2,1,0:T(8,128)} copy(f32[5,127,8,128]{3,2,1,0:T(8,128)S(1)} %bitcast.15) | data formatting | bytes 5201920
  61.5 1.5 %copy.20 = f32[5,127,8,128]{3,2,1,0:T(8,128)} copy(f32[5,127,8,128]{3,2,1,0:T(8,128)S(1)} %bitcast.14) | data formatting | bytes 5201920

commit v4 on v3

--- a/solution.py
+++ b/solution.py
@@ -20,6 +20,7 @@
 PAIRS = COMPS * ROWS // 2
 PACKED = [(q % COMPS) * ROWS + q // COMPS for q in range(COMPS * ROWS)]
 EDGE = 3 * 3 * COMPS
+EARLY = 3
 F32 = jnp.float32
 BF16 = jnp.bfloat16
 
@@ -351,6 +352,8 @@
         def _():
             corner_south(phase).start()
 
+        for k in range(EARLY, COMPS):
+            lat_start(phase, k)
         high, low = split(edges)
         edges = jnp.concatenate([high, low], 0)
         for p in range(PAIRS):
@@ -451,30 +454,44 @@
         return remote(rec_out2.at[pl.ds(0, LON - 1)], rec_in2.at[pl.ds(0, LON - 1)],
                       rec2_send.at[0], rec2_recv.at[0], "lon", lon_peer(1))
 
+    def weigh():
+        rec2_all().wait_recv()
+
+        records = rec_in2[...].reshape(LAT * LON * CAP, CELLS)
+        high, low = split(records.T)
+        rec_t[...] = jnp.concatenate([high, low], 0)
+        cell = records[:, LEV:].astype(jnp.int32)
+
+        @pl.loop(0, ROWS, unroll=4)
+        def _(p):
+            hit = cell == iota((LAT * LON * CAP, 2 * CELLS), 1) + p * 2 * CELLS
+            both = mxu(rec_t[...], jnp.where(hit, 1.0, 0.0).astype(BF16))
+            total = both[:CELLS] + both[CELLS:]
+            dens[2 * p] = total[:, :CELLS]
+            dens[2 * p + 1] = total[:, CELLS:]
+
     d_loads[0].wait()
     d_loads[1].wait()
     own_part(0, 0, d_rows)
-    build_selections()
+    pack_records()
     pl.semaphore_wait(barrier, LAT + LON - 2)
-    lat_start(0, 0)
-    pack_records()
 
     @pl.loop(1, LAT)
     def _(o):
         rec1(o).start()
 
+    lat_start(0, 0)
     rec_in1[lat] = rec_out1[lat]
     for copy in d_loads[2:]:
         copy.wait()
     own_part(0, 1, d_rows)
     lat_start(0, 1)
+    build_selections()
     pack_lon(0, d_rows)
     for copy in edge_copies(0):
         copy.start()
-    for k in range(2, COMPS):
-        own_part(0, k, d_rows)
-        lat_start(0, k)
-
+    own_part(0, 2, d_rows)
+    lat_start(0, 2)
     rec1_all().wait_recv()
 
     @pl.loop(0, LON // 2)
@@ -490,6 +507,8 @@
         rec2(o).start()
 
     rec_in2[lon] = rec_out2[lon]
+    for k in range(3, COMPS):
+        own_part(0, k, d_rows)
     lon_part(0)
     ens_load.wait()
 
@@ -513,38 +532,25 @@
         return total_r, total_d
 
     sum_r, sum_d = lax.fori_loop(0, LEV, squares, (zeros8, zeros8))
-    rec2_all().wait_recv()
-
-    records = rec_in2[...].reshape(LAT * LON * CAP, CELLS)
-    high, low = split(records.T)
-    rec_t[...] = jnp.concatenate([high, low], 0)
-    cell = records[:, LEV:].astype(jnp.int32)
-
-    @pl.loop(0, ROWS)
-    def _(p):
-        hit = cell == iota((LAT * LON * CAP, 2 * CELLS), 1) + p * 2 * CELLS
-        both = mxu(rec_t[...], jnp.where(hit, 1.0, 0.0).astype(BF16))
-        total = both[:CELLS] + both[CELLS:]
-        dens[2 * p] = total[:, :CELLS]
-        dens[2 * p + 1] = total[:, CELLS:]
-
     @pl.loop(0, 2 * ROWS)
     def _(q):
         inc[q] = jnp.zeros((CELLS, CELLS), F32)
 
     corner_part(0)
 
-    @pl.loop(0, MEMBERS)
-    def _(k):
+    def gather(k):
         lat_arrived(0, k)
 
-        @pl.loop(0, CELLS // 8)
+        @pl.loop(0, CELLS // 8, unroll=2)
         def _(c):
             rows = lat_rows(0, k, c)
             for t in range(2):
                 for i in range(ROWS):
                     inc[t * ROWS + i, pl.ds(c * 8, 8)] += ens_rows(2 * k + t, c, i) * rows[i]
 
+    pl.loop(0, 2)(gather)
+    weigh()
+    pl.loop(2, MEMBERS)(gather)
     lat_arrived(0, MEMBERS)
 
     def adjoint(c, curve):
@@ -565,11 +571,12 @@
             x_ref[MEMBERS * ROWS + i, part] = spread * (back0 + back1)
         return curve
 
-    curve = lax.fori_loop(0, CELLS // 8, adjoint, sum_d)
+    curve = lax.fori_loop(0, CELLS // 8, adjoint, sum_d, unroll=2)
     lat_sent(0)
     for k in range(COMPS):
         own_part(1, k, x_rows)
-        lat_start(1, k)
+        if k < EARLY:
+            lat_start(1, k)
         if k == 0:
             pack_lon(1, x_rows)
             for copy in edge_copies(1):
@@ -582,8 +589,8 @@
                 ),
             )
             reduce_first(0, sums)
+    lon_part(1)
     reduce_second(0)
-    lon_part(1)
     sums = reduce_last(0)
     norm_now = jnp.sum(sums[0:1], keepdims=True)
     alpha = norm_now / jnp.sum(sums[1:2], keepdims=True)
@@ -609,7 +616,7 @@
                 total[height] = total[height] + value * value
             return total
 
-        total = lax.fori_loop(0, LEV // 8, body, total)
+        total = lax.fori_loop(0, LEV // 8, body, total, unroll=3)
         return body(LEV // 8, total, LEV % 8)
 
     def finish(n, carry):
@@ -623,7 +630,7 @@
     reduce_second(1)
     norm_next = jnp.sum(reduce_last(1), keepdims=True)
     beta = norm_next / norm_now
-    lax.fori_loop(0, LEV, finish, 0)
+    lax.fori_loop(0, LEV, finish, 0, unroll=4)
 
     lat_sent(1)
     for phase in range(2):

time: 63.1 us -> 59.3 us (0.940)
  Pallas kernels: 57.3 us -> 53.4 us
    pallas_call x1, Pallas kernels: 57.3 us -> 53.4 us  [on_device(): pl.pallas_call(kernel, out_shape=(pltpu.VMEM(flat, F32),) * 3, in_specs=[...]
where the time goes in v4:
time: 59.3 us; the launch traced here: 59.1 us
  Pallas kernels  53.4 us (90%)
  local copies, waits for them, and re-layouts  4.46 us (8%)
  between operations  1.29 us (2%)
    pallas_call x1, Pallas kernels, on_device(): pl.pallas_call(kernel, out_shape=(pltpu.VMEM(flat, F32),) * 3, in_specs=[...  53.4 us
    unnamed x3, local copies, waits for them, and re-layouts  4.46 us

profile of v4, /device:TPU:1, one launch (start us, length us, event | category | flops | bytes accessed | tf_op | source)
XLA Modules:
  0.0 59.1 jit_solution(10450989900749090093)
XLA Ops:
  1.3 53.4 %analysis_step.1 = (f32[5080,128]{1,0:T(8,128)S(1)}, f32[5080,128]{1,0:T(8,128)S(1)}, f32[5080,128]{1,0:T(8,128)S(1)}) custom-call(s32[1,1]{1,0:T(1,128)} %bitcast.13.live_hbm, s32[1,256]{1,0:T(1,128)} %bitcast.23, s32[1,256]{1,0:T(1,128)} %bitcast.24, s32[1,256]{1,0:T(1,128)} %bitcast.25, s32[4,256]{1,0:T(4,128)} %bitcast.22, f32[256,127]{1,0:T(8,128)} %weight_hbm.1, ...), custom_call_target="tpu_custom_call" | custom-call | tf_op jit(solution)/shard_map/analysis_step/pallas_call | solution.py:664
  54.7 1.5 %copy.18 = f32[5,127,8,128]{3,2,1,0:T(8,128)} copy(f32[5,127,8,128]{3,2,1,0:T(8,128)S(1)} %bitcast.16) | data formatting | bytes 5201920
  56.2 1.5 %copy.19 = f32[5,127,8,128]{3,2,1,0:T(8,128)} copy(f32[5,127,8,128]{3,2,1,0:T(8,128)S(1)} %bitcast.15) | data formatting | bytes 5201920
  57.7 1.5 %copy.20 = f32[5,127,8,128]{3,2,1,0:T(8,128)} copy(f32[5,127,8,128]{3,2,1,0:T(8,128)S(1)} %bitcast.14) | data formatting | bytes 5201920

commit v5 on v4

--- a/solution.py
+++ b/solution.py
@@ -595,13 +595,6 @@
     norm_now = jnp.sum(sums[0:1], keepdims=True)
     alpha = norm_now / jnp.sum(sums[1:2], keepdims=True)
 
-    c_load.wait()
-
-    @pl.loop(0, LEV)
-    def _(n):
-        part = pl.ds(n * 40, 40)
-        control_ref[part, :] = c_nat[part, :] + alpha * d_nat[part, :]
-
     corner_part(1)
 
     def update(k, total):
@@ -627,11 +620,15 @@
     total = lax.fori_loop(0, COMPS, update, {8: zeros8, 7: zeros8[:7]})
     last = jnp.concatenate([total[7], jnp.zeros((1, CELLS), F32)], 0)
     reduce_first(1, total[8] + last)
+
+    c_load.wait()
+
+    @pl.loop(0, LEV)
+    def _(n):
+        part = pl.ds(n * 40, 40)
+        control_ref[part, :] = c_nat[part, :] + alpha * d_nat[part, :]
+
     reduce_second(1)
-    norm_next = jnp.sum(reduce_last(1), keepdims=True)
-    beta = norm_next / norm_now
-    lax.fori_loop(0, LEV, finish, 0, unroll=4)
-
     lat_sent(1)
     for phase in range(2):
         for copy in edge_copies(phase):
@@ -645,10 +642,16 @@
         def _():
             corner_south(phase).wait_send()
 
-        first_all(phase).wait_send()
-        second_all(phase).wait_send()
+    first_all(0).wait_send()
+    second_all(0).wait_send()
     rec1_all().wait_send()
     rec2_all().wait_send()
+
+    norm_next = jnp.sum(reduce_last(1), keepdims=True)
+    beta = norm_next / norm_now
+    lax.fori_loop(0, LEV, finish, 0, unroll=4)
+    first_all(1).wait_send()
+    second_all(1).wait_send()
 
 
 def on_device(

time: 59.3 us -> 58.3 us (0.983)
  Pallas kernels: 53.4 us -> 52.5 us
    pallas_call x1, Pallas kernels: 53.4 us -> 52.5 us  [on_device(): pl.pallas_call(kernel, out_shape=(pltpu.VMEM(flat, F32),) * 3, in_specs=[...]
where the time goes in v5:
time: 58.3 us; the launch traced here: 58.2 us
  Pallas kernels  52.5 us (90%)
  local copies, waits for them, and re-layouts  4.46 us (8%)
  between operations  1.29 us (2%)
    pallas_call x1, Pallas kernels, on_device(): pl.pallas_call(kernel, out_shape=(pltpu.VMEM(flat, F32),) * 3, in_specs=[...  52.5 us
    unnamed x3, local copies, waits for them, and re-layouts  4.46 us

profile of v5, /device:TPU:1, one launch (start us, length us, event | category | flops | bytes accessed | tf_op | source)
XLA Modules:
  0.0 58.2 jit_solution(8530648851604590506)
XLA Ops:
  1.3 52.5 %analysis_step.1 = (f32[5080,128]{1,0:T(8,128)S(1)}, f32[5080,128]{1,0:T(8,128)S(1)}, f32[5080,128]{1,0:T(8,128)S(1)}) custom-call(s32[1,1]{1,0:T(1,128)} %bitcast.13.live_hbm, s32[1,256]{1,0:T(1,128)} %bitcast.23, s32[1,256]{1,0:T(1,128)} %bitcast.24, s32[1,256]{1,0:T(1,128)} %bitcast.25, s32[4,256]{1,0:T(4,128)} %bitcast.22, f32[256,127]{1,0:T(8,128)} %weight_hbm.1, ...), custom_call_target="tpu_custom_call" | custom-call | tf_op jit(solution)/shard_map/analysis_step/pallas_call | solution.py:667
  53.8 1.5 %copy.18 = f32[5,127,8,128]{3,2,1,0:T(8,128)} copy(f32[5,127,8,128]{3,2,1,0:T(8,128)S(1)} %bitcast.16) | data formatting | bytes 5201920
  55.2 1.5 %copy.19 = f32[5,127,8,128]{3,2,1,0:T(8,128)} copy(f32[5,127,8,128]{3,2,1,0:T(8,128)S(1)} %bitcast.15) | data formatting | bytes 5201920
  56.7 1.5 %copy.20 = f32[5,127,8,128]{3,2,1,0:T(8,128)} copy(f32[5,127,8,128]{3,2,1,0:T(8,128)S(1)} %bitcast.14) | data formatting | bytes 5201920
